TPU v7x, 128 devices: a whole 4x4x4 slice. The times are simulated.
128 devices in a mesh: seq: 16 (over y, z_lo, core), chan: 8 (over z_hi, x).
Axes of the slice: x: 4, y: 4, z: 4 (z_hi: 2, z_lo: 2; z = z_hi * 2 + z_lo), core: 2. Of those that a mesh axis runs over, the one named last changes fastest.
Arguments:
- stream_one: bfloat16 [4096, 8192], P('chan', 'seq'), may hold values from -6 to 6
- stream_two: bfloat16 [4096, 8192], P('chan', 'seq'), may hold values from -6 to 6
- stream_value: bfloat16 [4096, 8192], P('chan', 'seq'), may hold values from -6 to 6
- grad_output: bfloat16 [4096, 8192], P('chan', 'seq'), may hold values from -6 to 6
- long_taps: bfloat16 [4096, 8192], P('chan', 'seq'), may hold values from -0.0625 to 0.0625
- short_taps: float32 [3, 3, 4096], P(None, None, 'chan'), may hold values from -3.5 to 3.5
- skip_gain: float32 [4096], P('chan'), may hold values from 0.25 to 1.5
- sketch_matrix: bfloat16 [1024, 8192], P(None, 'seq'), may hold values from -0.0007324219 to 0.0007324219
Outputs:
- grad_one: bfloat16 [4096, 8192], P('chan', 'seq')
- grad_two: bfloat16 [4096, 8192], P('chan', 'seq')
- grad_value: bfloat16 [4096, 8192], P('chan', 'seq')
- saliency: float32 [8192], P(('seq', 'chan'))
- sketch: float32 [1024, 4096], P('seq', 'chan')
All inputs are finite; a program needn't handle non-finite values.
Results may differ from a plain program's by a relative error of at most 0.0057.
Values may be sent and summed in bfloat16 or wider, within the bound.
A program may use at most 128 MiB of HBM per device.

v0:
```python
import math

import jax
import jax.numpy as jnp
from jax import lax
from jax.sharding import PartitionSpec as P

D = 4096


def delay(field, steps):
    return jnp.pad(field[:, : field.shape[1] - steps], ((0, 0), (steps, 0)))


def advance(field, steps):
    return jnp.pad(field[:, steps:], ((0, 0), (0, steps)))


def causal_short(field, weights):
    return (
        weights[0][:, None] * field
        + weights[1][:, None] * delay(field, 1)
        + weights[2][:, None] * delay(field, 2)
    )


def adjoint_short(field, weights):
    return (
        weights[0][:, None] * field
        + weights[1][:, None] * advance(field, 1)
        + weights[2][:, None] * advance(field, 2)
    )


def build_tables(half):
    twice = 2 * half
    total_len = twice * 128
    outer = jnp.arange(twice, dtype=jnp.int32)
    inner = jnp.arange(half, dtype=jnp.int32)
    lanes = jnp.arange(128, dtype=jnp.int32)
    first_angle = (
        2.0 * math.pi / twice * (outer[:, None] * inner[None, :] % twice).astype(jnp.float32)
    )
    twist_angle = (
        2.0
        * math.pi
        / total_len
        * (outer[:, None] * lanes[None, :] % total_len).astype(jnp.float32)
    )
    last_angle = 2.0 * math.pi / 128 * (lanes[:, None] * lanes[None, :] % 128).astype(jnp.float32)
    return (
        jnp.cos(first_angle),
        jnp.sin(first_angle),
        jnp.cos(twist_angle),
        jnp.sin(twist_angle),
        jnp.cos(last_angle),
        jnp.sin(last_angle),
    )


def product(form, left, right):
    return jnp.einsum(form, left, right, precision=lax.Precision.HIGH)


def spectrum(signal, tables):
    first_cos, first_sin, twist_cos, twist_sin, last_cos, last_sin = tables
    real_a = product("ka,cab->ckb", first_cos, signal)
    imag_a = -product("ka,cab->ckb", first_sin, signal)
    real_b = real_a * twist_cos + imag_a * twist_sin
    imag_b = imag_a * twist_cos - real_a * twist_sin
    real_c = product("ckb,bm->ckm", real_b, last_cos) + product("ckb,bm->ckm", imag_b, last_sin)
    imag_c = product("ckb,bm->ckm", imag_b, last_cos) - product("ckb,bm->ckm", real_b, last_sin)
    return (real_c, imag_c)


def restore(real_c, imag_c, tables):
    first_cos, first_sin, twist_cos, twist_sin, last_cos, last_sin = tables
    real_e = product("ckm,mb->ckb", real_c, last_cos) - product("ckm,mb->ckb", imag_c, last_sin)
    imag_e = product("ckm,mb->ckb", imag_c, last_cos) + product("ckm,mb->ckb", real_c, last_sin)
    real_f = real_e * twist_cos - imag_e * twist_sin
    imag_f = imag_e * twist_cos + real_e * twist_sin
    total_len = twist_cos.shape[0] * 128
    value = product("ka,ckb->cab", first_cos, real_f) - product("ka,ckb->cab", first_sin, imag_f)
    return value / total_len


def on_device(
    stream_one,
    stream_two,
    stream_value,
    grad_output,
    long_taps,
    short_taps,
    skip_gain,
    sketch_matrix,
):
    seq_count = lax.axis_size("seq")
    width_dev = stream_one.shape[0]
    group = width_dev // seq_count
    moved = (
        lax.all_to_all(stream_one, "seq", split_axis=0, concat_axis=1, tiled=True),
        lax.all_to_all(stream_two, "seq", split_axis=0, concat_axis=1, tiled=True),
        lax.all_to_all(stream_value, "seq", split_axis=0, concat_axis=1, tiled=True),
        lax.all_to_all(grad_output, "seq", split_axis=0, concat_axis=1, tiled=True),
        lax.all_to_all(long_taps, "seq", split_axis=0, concat_axis=1, tiled=True),
    )
    length = moved[0].shape[1]
    half = length // 128
    first_in = moved[0].astype(jnp.float32)
    second_in = moved[1].astype(jnp.float32)
    value_in = moved[2].astype(jnp.float32)
    grad_in = moved[3].astype(jnp.float32)
    offset = lax.axis_index("seq") * group
    conv_taps = lax.dynamic_slice_in_dim(short_taps, offset, group, 2)
    gains = lax.dynamic_slice_in_dim(skip_gain, offset, group, 0)[:, None]
    act_one = causal_short(first_in, conv_taps[0])
    act_two = causal_short(second_in, conv_taps[1])
    act_value = causal_short(value_in, conv_taps[2])
    gated = (act_two * act_value).astype(jnp.bfloat16)
    gated_wide = lax.optimization_barrier(gated).astype(jnp.float32)
    grad_gate = (grad_in * act_one).astype(jnp.bfloat16)
    grad_gate_wide = lax.optimization_barrier(grad_gate).astype(jnp.float32)
    tables = build_tables(half)

    def to_grid(field):
        return field.reshape(group, half, 128)

    def from_grid(grid):
        return grid.reshape(group, length)

    filter_re, filter_im = spectrum(to_grid(moved[4].astype(jnp.float32)), tables)
    gate_re, gate_im = spectrum(to_grid(gated_wide), tables)
    grad_re, grad_im = spectrum(to_grid(grad_gate_wide), tables)
    mixed = (
        from_grid(
            restore(
                filter_re * gate_re - filter_im * gate_im,
                filter_re * gate_im + filter_im * gate_re,
                tables,
            )
        )
        + gains * gated_wide
    )
    grad_mix = (
        from_grid(
            restore(
                filter_re * grad_re + filter_im * grad_im,
                filter_re * grad_im - filter_im * grad_re,
                tables,
            )
        )
        + gains * grad_gate_wide
    )
    grad_filter = from_grid(
        restore(
            gate_re * grad_re + gate_im * grad_im, gate_re * grad_im - gate_im * grad_re, tables
        )
    ).astype(jnp.bfloat16)
    full_one = adjoint_short(grad_in * mixed, conv_taps[0])
    full_two = adjoint_short(grad_mix * act_value, conv_taps[1])
    full_value = adjoint_short(grad_mix * act_two, conv_taps[2])
    attrib = jnp.sum(first_in * full_one + second_in * full_two + value_in * full_value, axis=0)
    saliency = lax.psum_scatter(attrib, ("seq", "chan"), scatter_dimension=0, tiled=True) * (
        3.0 * D
    ) ** (-0.5)
    narrow_one = full_one.astype(jnp.bfloat16)
    narrow_two = full_two.astype(jnp.bfloat16)
    narrow_value = full_value.astype(jnp.bfloat16)
    whole_sketch = lax.dot_general(
        lax.all_gather(sketch_matrix, "seq", axis=1, tiled=True),
        grad_filter,
        (((1,), (1,)), ((), ())),
        preferred_element_type=jnp.float32,
    )
    sketch = lax.all_to_all(whole_sketch, "seq", split_axis=0, concat_axis=1, tiled=True)
    grad_one, grad_two, grad_value = (
        lax.all_to_all(narrow_one, "seq", split_axis=1, concat_axis=0, tiled=True),
        lax.all_to_all(narrow_two, "seq", split_axis=1, concat_axis=0, tiled=True),
        lax.all_to_all(narrow_value, "seq", split_axis=1, concat_axis=0, tiled=True),
    )
    return (grad_one, grad_two, grad_value, saliency, sketch)


def solution(mesh):
    return jax.shard_map(
        on_device,
        mesh=mesh,
        in_specs=(
            P("chan", "seq"),
            P("chan", "seq"),
            P("chan", "seq"),
            P("chan", "seq"),
            P("chan", "seq"),
            P(None, None, "chan"),
            P("chan"),
            P(None, "seq"),
        ),
        out_specs=(
            P("chan", "seq"),
            P("chan", "seq"),
            P("chan", "seq"),
            P(("seq", "chan")),
            P("seq", "chan"),
        ),
        check_vma=False,
    )
```

profile of v0, /device:TPU:1, one launch (start us, length us, event | category | flops | bytes accessed | tf_op | source)
XLA Modules:
  0.0 300.6 jit_solution(1095126897551913588)
XLA Ops:
  7.9 17.0 %all_to_all.144 = bf16[16,32,512]{2,1,0:T(8,128)(2,1)S(1)} all-to-all(bf16[16,32,512]{2,1,0:T(8,128)(2,1)} %bitcast.295), channel_id=1, replica_groups=mesh['seq'=16,'chan'=8] {'seq'}, dimensions={0} | all-to-all | bytes 1048576 | tf_op jit(solution)/shard_map/all_to_all | solution.py:101
  24.9 4.7 %all-to-all-start = ((bf16[16,32,512]{2,1,0:T(8,128)(2,1)}), bf16[16,32,512]{2,1,0:T(8,128)(2,1)S(1)}, u32[]{:S(2)}, u32[]{:S(2)}) async-start(bf16[16,32,512]{2,1,0:T(8,128)(2,1)} %bitcast.1), calls=%async_computation | async-start | bytes 1048576 | tf_op jit(solution)/shard_map/all_to_all | solution.py:104
  31.7 12.3 %all-to-all-done = bf16[16,32,512]{2,1,0:T(8,128)(2,1)S(1)} async-done(((bf16[16,32,512]{2,1,0:T(8,128)(2,1)}), bf16[16,32,512]{2,1,0:T(8,128)(2,1)S(1)}, u32[]{:S(2)}, u32[]{:S(2)}) %all-to-all-start) | async-done | bytes 524320 | tf_op jit(solution)/shard_map/all_to_all | solution.py:104
  44.0 5.1 %all-to-all-start.3 = ((bf16[16,32,512]{2,1,0:T(8,128)(2,1)}), bf16[16,32,512]{2,1,0:T(8,128)(2,1)S(1)}, u32[]{:S(2)}, u32[]{:S(2)}) async-start(bf16[16,32,512]{2,1,0:T(8,128)(2,1)} %bitcast.17), calls=%async_computation.3 | async-start | bytes 1048576 | tf_op jit(solution)/shard_map/all_to_all | solution.py:103
  49.6 13.9 %all-to-all-done.3 = bf16[16,32,512]{2,1,0:T(8,128)(2,1)S(1)} async-done(((bf16[16,32,512]{2,1,0:T(8,128)(2,1)}), bf16[16,32,512]{2,1,0:T(8,128)(2,1)S(1)}, u32[]{:S(2)}, u32[]{:S(2)}) %all-to-all-start.3) | async-done | bytes 524320 | tf_op jit(solution)/shard_map/all_to_all | solution.py:103
  63.5 5.1 %all-to-all-start.2 = ((bf16[16,32,512]{2,1,0:T(8,128)(2,1)}), bf16[16,32,512]{2,1,0:T(8,128)(2,1)S(1)}, u32[]{:S(2)}, u32[]{:S(2)}) async-start(bf16[16,32,512]{2,1,0:T(8,128)(2,1)} %bitcast.296), calls=%async_computation.2 | async-start | bytes 1048576 | tf_op jit(solution)/shard_map/all_to_all | solution.py:102
  68.6 1.4 multiply_convert_fusion
  70.0 13.0 %all-to-all-done.2 = bf16[16,32,512]{2,1,0:T(8,128)(2,1)S(1)} async-done(((bf16[16,32,512]{2,1,0:T(8,128)(2,1)}), bf16[16,32,512]{2,1,0:T(8,128)(2,1)S(1)}, u32[]{:S(2)}, u32[]{:S(2)}) %all-to-all-start.2) | async-done | bytes 524320 | tf_op jit(solution)/shard_map/all_to_all | solution.py:102
  83.0 5.3 %all-to-all-start.1 = ((bf16[16,32,512]{2,1,0:T(8,128)(2,1)}), bf16[16,32,512]{2,1,0:T(8,128)(2,1)}, u32[]{:S(2)}, u32[]{:S(2)}) async-start(bf16[16,32,512]{2,1,0:T(8,128)(2,1)} %bitcast.297), calls=%async_computation.1 | async-start | bytes 1048576 | tf_op jit(solution)/shard_map/all_to_all | solution.py:105
  90.4 12.1 %all-to-all-done.1 = bf16[16,32,512]{2,1,0:T(8,128)(2,1)} async-done(((bf16[16,32,512]{2,1,0:T(8,128)(2,1)}), bf16[16,32,512]{2,1,0:T(8,128)(2,1)}, u32[]{:S(2)}, u32[]{:S(2)}) %all-to-all-start.1) | async-done | bytes 524320 | tf_op jit(solution)/shard_map/all_to_all | solution.py:105
  102.6 2.1 copy.89
  104.7 2.2 reshape.127
  106.9 2.2 fusion.147
  111.9 2.1 fusion.90
  114.0 2.1 fusion.86
  116.1 1.4 fusion.6
  117.6 1.4 fusion.4
  119.0 2.4 convolution_add_fusion.2
  121.3 1.5 fusion.36
  122.8 2.1 convolution_subtract_fusion.2
  125.0 1.9 multiply_subtract_fusion.1
  130.7 1.3 convolution_add_fusion.1
  132.0 1.9 fusion.20
  133.9 1.5 fusion.54
  135.4 1.9 fusion.77
  137.6 1.3 slice.127
  138.9 1.3 slice.126
  140.2 1.4 slice.125
  143.9 2.1 fusion.84
  146.0 2.1 fusion.80
  148.1 2.3 convolution_add_fusion.4
  150.4 4.6 %multiply_subtract_fusion = (f32[32,128,128]{2,1,0:T(8,128)}, f32[32,128,128]{2,1,0:T(8,128)}, f32[32,128,128]{2,1,0:T(8,128)S(1)}, f32[32,128,128]{2,1,0:T(8,128)S(1)}) fusion(f32[32,128,128]{2,1,0:T(8,128)S(1)} %convolution_add_fusion.2, f32[32,128,128]{2,1,0:T(8,128)S(1)} %convolution_add_fusion.4, f32[32,128,128]{2,1,0:T(8,128)S(1)} %convolution_subtract_fusion.2, ...), kind=kOutput, calls=%fused_computation.28 | convolution fusion | flops 411795456 | bytes 25296896 | tf_op jit(solution)/shard_map/ckb,bm->ckm/dot_general | solution.py:62
  157.5 1.3 convolution_subtract_fusion.3
  158.8 1.3 convolution_add_fusion.3
  160.1 1.5 fusion.28
  161.5 1.5 fusion.57
  165.6 2.4 add_reduce_fusion
  168.8 5.2 %all-to-all-start.4 = ((bf16[32,16,512]{2,0,1:T(8,128)(2,1)}), bf16[32,16,512]{2,0,1:T(8,128)(2,1)S(1)}, u32[]{:S(2)}, u32[]{:S(2)}) async-start(bf16[32,16,512]{2,0,1:T(8,128)(2,1)} %bitcast.256), calls=%async_computation.4 | async-start | bytes 1048576 | tf_op jit(solution)/shard_map/all_to_all | solution.py:177
  175.6 2.7 convolution_subtract_fusion
  180.4 2.6 convolution_add_fusion
  183.5 5.2 %all-to-all-start.6 = ((bf16[32,16,512]{2,0,1:T(8,128)(2,1)}), bf16[32,16,512]{2,0,1:T(8,128)(2,1)S(1)}, u32[]{:S(2)}, u32[]{:S(2)}) async-start(bf16[32,16,512]{2,0,1:T(8,128)(2,1)} %bitcast.255), calls=%async_computation.6 | async-start | bytes 1048576 | tf_op jit(solution)/shard_map/all_to_all | solution.py:178
  188.8 3.8 %fusion.12 = f32[32,128,64]{1,2,0:T(8,128)S(1)} fusion(f32[32,128,128]{1,2,0:T(8,128)} %convolution_subtract_fusion, f32[32,128,128]{1,2,0:T(8,128)} %convolution_add_fusion, f32[128,128]{0,1:T(8,128)S(1)} %copy.93, f32[128,128]{0,1:T(8,128)S(1)} %copy.92), kind=kOutput, calls=%fused_computation.20 | convolution fusion | flops 203014144 | bytes 5373952 | tf_op jit(solution)/shard_map/ka,ckb->cab/dot_general | solution.py:62
  193.4 1.5 fusion.60
  194.9 3.5 %all-to-all-done.6 = bf16[32,16,512]{2,0,1:T(8,128)(2,1)S(1)} async-done(((bf16[32,16,512]{2,0,1:T(8,128)(2,1)}), bf16[32,16,512]{2,0,1:T(8,128)(2,1)S(1)}, u32[]{:S(2)}, u32[]{:S(2)}) %all-to-all-start.6) | async-done | bytes 524320 | tf_op jit(solution)/shard_map/all_to_all | solution.py:178
  198.4 4.7 %all-to-all-start.7 = ((bf16[32,16,512]{2,0,1:T(8,128)(2,1)}), bf16[32,16,512]{2,0,1:T(8,128)(2,1)S(1)}, u32[]{:S(2)}, u32[]{:S(2)}) async-start(bf16[32,16,512]{2,0,1:T(8,128)(2,1)} %bitcast.254), calls=%async_computation.7 | async-start | bytes 1048576 | tf_op jit(solution)/shard_map/all_to_all | solution.py:179
  203.1 10.8 %convolution_bitcast_fusion = f32[1024,32]{0,1:T(8,128)S(1)} fusion(bf16[1024,8192]{1,0:T(8,128)(2,1)} %all-gather.2.cloned.1.call-done, bf16[4,8,64,128]{3,2,1,0:T(8,128)(2,1)S(1)} %bitcast.286), kind=kOutput, calls=%fused_computation.71 | convolution fusion | flops 536870912 | bytes 17432576 | tf_op jit(solution)/shard_map/dot_general | solution.py:169
  214.9 5.8 %all-to-all-start.8 = ((f32[16,1,2048]{2,1,0:T(1,128)}), f32[16,1,2048]{2,1,0:T(1,128)S(1)}, u32[]{:S(2)}, u32[]{:S(2)}) async-start(f32[16,1,2048]{2,1,0:T(1,128)} %reshape.140), calls=%async_computation.8 | async-start | bytes 262144 | tf_op jit(solution)/shard_map/all_to_all | solution.py:175
  220.7 67.5 %all-reduce.12 = f32[8192]{0:T(1024)S(1)} all-reduce(f32[8192]{0:T(1024)S(1)} %get-tuple-element.15), channel_id=2, replica_groups=mesh['seq'=16,'chan'=8] {'seq','chan'}, use_global_device_ids=true, to_apply=%region_1.2.clone | all-reduce | flops 8192 | bytes 65536
  (82 shorter events, 31.9 us)
Async XLA Ops:
  7.2 195.9 %all-gather.2.cloned.1.call-start = ((), (), s32[]{:S(2)}) async-start(), calls=%async_computation.9 | async-start | bytes 17825792 | tf_op jit(solution)/shard_map/all_gather | solution.py:170
  24.9 19.1 %all-to-all-start = ((bf16[16,32,512]{2,1,0:T(8,128)(2,1)}), bf16[16,32,512]{2,1,0:T(8,128)(2,1)S(1)}, u32[]{:S(2)}, u32[]{:S(2)}) async-start(bf16[16,32,512]{2,1,0:T(8,128)(2,1)} %bitcast.1), calls=%async_computation | async-start | bytes 1048576 | tf_op jit(solution)/shard_map/all_to_all | solution.py:104
  44.0 19.5 %all-to-all-start.3 = ((bf16[16,32,512]{2,1,0:T(8,128)(2,1)}), bf16[16,32,512]{2,1,0:T(8,128)(2,1)S(1)}, u32[]{:S(2)}, u32[]{:S(2)}) async-start(bf16[16,32,512]{2,1,0:T(8,128)(2,1)} %bitcast.17), calls=%async_computation.3 | async-start | bytes 1048576 | tf_op jit(solution)/shard_map/all_to_all | solution.py:103
  49.6 20.5 %copy-start.4 = (f32[16,4,8,512]{3,2,0,1:T(8,128)}, f32[16,4,8,512]{3,2,0,1:T(8,128)S(1)}, u32[]{:S(2)}) copy-start(f32[16,4,8,512]{3,2,0,1:T(8,128)S(1)} %copy.155) | copy-start | bytes 3145732
  63.5 19.5 %all-to-all-start.2 = ((bf16[16,32,512]{2,1,0:T(8,128)(2,1)}), bf16[16,32,512]{2,1,0:T(8,128)(2,1)S(1)}, u32[]{:S(2)}, u32[]{:S(2)}) async-start(bf16[16,32,512]{2,1,0:T(8,128)(2,1)} %bitcast.296), calls=%async_computation.2 | async-start | bytes 1048576 | tf_op jit(solution)/shard_map/all_to_all | solution.py:102
  83.0 19.6 %all-to-all-start.1 = ((bf16[16,32,512]{2,1,0:T(8,128)(2,1)}), bf16[16,32,512]{2,1,0:T(8,128)(2,1)}, u32[]{:S(2)}, u32[]{:S(2)}) async-start(bf16[16,32,512]{2,1,0:T(8,128)(2,1)} %bitcast.297), calls=%async_computation.1 | async-start | bytes 1048576 | tf_op jit(solution)/shard_map/all_to_all | solution.py:105
  88.5 1.1 copy-start.8
  106.9 2.2 copy-start.6
  106.9 3.2 %copy-start.7 = (bf16[32,64,128]{2,1,0:T(8,128)(2,1)S(1)}, bf16[32,64,128]{2,1,0:T(8,128)(2,1)}, u32[]{:S(2)}) copy-start(bf16[32,64,128]{2,1,0:T(8,128)(2,1)} %reshape.127) | copy-start | bytes 1572868
  133.9 1.5 copy-start.9
  161.5 1.5 copy-start.5
  163.7 1.2 copy-start.10
  163.7 1.5 copy-start.11
  163.7 1.8 copy-start.12
  167.9 6.1 %copy-start = (f32[32,128,128]{2,1,0:T(8,128)S(1)}, f32[32,128,128]{2,1,0:T(8,128)}, u32[]{:S(2)}) copy-start(f32[32,128,128]{2,1,0:T(8,128)} %get-tuple-element.24) | copy-start | bytes 6291460
  168.8 14.8 %all-to-all-start.4 = ((bf16[32,16,512]{2,0,1:T(8,128)(2,1)}), bf16[32,16,512]{2,0,1:T(8,128)(2,1)S(1)}, u32[]{:S(2)}, u32[]{:S(2)}) async-start(bf16[32,16,512]{2,0,1:T(8,128)(2,1)} %bitcast.256), calls=%async_computation.4 | async-start | bytes 1048576 | tf_op jit(solution)/shard_map/all_to_all | solution.py:177
  174.0 1.6 copy-start.1
  178.3 1.3 copy-start.14
  183.5 14.8 %all-to-all-start.6 = ((bf16[32,16,512]{2,0,1:T(8,128)(2,1)}), bf16[32,16,512]{2,0,1:T(8,128)(2,1)S(1)}, u32[]{:S(2)}, u32[]{:S(2)}) async-start(bf16[32,16,512]{2,0,1:T(8,128)(2,1)} %bitcast.255), calls=%async_computation.6 | async-start | bytes 1048576 | tf_op jit(solution)/shard_map/all_to_all | solution.py:178
  188.7 3.8 %copy-start.13 = (bf16[32,8192]{1,0:T(8,128)(2,1)S(1)}, bf16[32,8192]{1,0:T(8,128)(2,1)}, u32[]{:S(2)}) copy-start(bf16[32,8192]{1,0:T(8,128)(2,1)} %get-tuple-element.16) | copy-start | bytes 1572868
  188.8 4.7 %copy-start.2 = (f32[32,128,128]{1,2,0:T(8,128)S(1)}, f32[32,128,128]{1,2,0:T(8,128)}, u32[]{:S(2)}) copy-start(f32[32,128,128]{1,2,0:T(8,128)} %convolution_subtract_fusion) | copy-start | bytes 6291460
  188.8 4.7 %copy-start.3 = (f32[32,128,128]{1,2,0:T(8,128)S(1)}, f32[32,128,128]{1,2,0:T(8,128)}, u32[]{:S(2)}) copy-start(f32[32,128,128]{1,2,0:T(8,128)} %convolution_add_fusion) | copy-start | bytes 6291460
  198.4 16.6 %all-to-all-start.7 = ((bf16[32,16,512]{2,0,1:T(8,128)(2,1)}), bf16[32,16,512]{2,0,1:T(8,128)(2,1)S(1)}, u32[]{:S(2)}, u32[]{:S(2)}) async-start(bf16[32,16,512]{2,0,1:T(8,128)(2,1)} %bitcast.254), calls=%async_computation.7 | async-start | bytes 1048576 | tf_op jit(solution)/shard_map/all_to_all | solution.py:179
  214.9 73.8 %all-to-all-start.8 = ((f32[16,1,2048]{2,1,0:T(1,128)}), f32[16,1,2048]{2,1,0:T(1,128)S(1)}, u32[]{:S(2)}, u32[]{:S(2)}) async-start(f32[16,1,2048]{2,1,0:T(1,128)} %reshape.140), calls=%async_computation.8 | async-start | bytes 262144 | tf_op jit(solution)/shard_map/all_to_all | solution.py:175
Sparse Core Ops, SparseCore 0:
  9.7 118.7 all-gather.1
where the time goes:
time: 305 us; the launch traced here: 301 us
  blocking collectives  84.5 us (28%)
  matrix products  73.3 us (24%)
  waiting for transfers between devices  55.9 us (18%)
  starting transfers between devices  41.1 us (13%)
  local copies, waits for them, and re-layouts  22.3 us (7%)
  between operations  14.8 us (5%)
  other arithmetic  8.73 us (3%)
    unnamed x1, blocking collectives  67.5 us
    dot_general x36, matrix products, product(): return jnp.einsum(form, left, right, precision=lax.Precision.HIGH)  62.5 us
    all_to_all x1, blocking collectives, on_device(): lax.all_to_all(stream_one, 'seq', split_axis=0, concat_axis=1, tiled=True)  17 us
    all_to_all x1, waiting for transfers between devices, on_device(): lax.all_to_all(stream_value, 'seq', split_axis=0, concat_axis=1, tiled=True)  13.9 us
    all_to_all x1, waiting for transfers between devices, on_device(): lax.all_to_all(stream_two, 'seq', split_axis=0, concat_axis=1, tiled=True)  13 us
    all_to_all x1, waiting for transfers between devices, on_device(): lax.all_to_all(grad_output, 'seq', split_axis=0, concat_axis=1, tiled=True)  12.3 us
    all_to_all x1, waiting for transfers between devices, on_device(): lax.all_to_all(long_taps, 'seq', split_axis=0, concat_axis=1, tiled=True)  12.1 us
    dot_general x1, matrix products, on_device(): lax.dot_general(lax.all_gather(sketch_matrix, 'seq', axis=1, tiled=True),...  10.8 us
  transfers between devices with their start and end apart: 9, of which 6 were waited for; matrix products, arithmetic and copies ran while one was open for 32% of the time, Pallas kernels for 0%

commit v1 on v0

v1 whole, which is shorter than its diff:
```python
import functools
import math

import jax
import jax.numpy as jnp
import numpy as np
from jax import lax
from jax.experimental import pallas as pl
from jax.experimental.pallas import tpu as pltpu
from jax.sharding import PartitionSpec as P

D = 4096
MESH = pl.DeviceIdType.MESH
F32 = jnp.float32
BF16 = jnp.bfloat16
ROOT = math.sqrt(0.5)
FREQS = [k1 + 32 * q for k1 in range(1, 16) for q in range(4)] + [0, 32, 64, 16, 48]
ROWS = 32 * len(FREQS)
CHUNK = 416


def split_host(table):
    high = table.astype(jnp.bfloat16)
    low = (table - high.astype(np.float64)).astype(jnp.bfloat16)
    return high, low


def host_tables():
    shard = np.arange(16)
    k1 = np.arange(16)
    first = np.zeros((4, 32, 16))
    for tile in range(4):
        angle = 2 * np.pi * np.outer(k1, 4 * shard + tile) / 128
        first[tile, :16] = np.cos(angle)
        first[tile, 16:] = -np.sin(angle)
        first[tile, 16] = (-1.0) ** shard
    eye = np.eye(16)
    wide = np.einsum("tks,cd->tkcsd", first, eye).reshape(4, 512, 256)
    back = np.einsum("tks,cd->tsckd", first, eye).reshape(4, 256, 512) * (2.0 / 16384)
    lane = np.arange(128)
    angle = 2 * np.pi * np.outer(lane, lane) / 128
    cos, sin = np.cos(angle), np.sin(angle)
    inner = np.block([[cos, -sin], [sin, cos]])
    inner_back = np.block([[cos, sin], [-sin, cos]])
    twist = 2 * np.pi * np.outer(np.array(FREQS + [0] * 7), lane) / 16384
    twist = np.concatenate([twist, twist], axis=1)
    return (
        *split_host(wide),
        *split_host(back),
        *split_host(inner),
        *split_host(inner_back),
        np.cos(twist).astype(np.float32),
        np.sin(twist).astype(np.float32),
    )


def dot(left, right):
    return jnp.dot(left, right, preferred_element_type=F32)


def dot_nt(left, right):
    return lax.dot_general(left, right, (((1,), (1,)), ((), ())), preferred_element_type=F32)


def halves(value):
    high = value.astype(BF16)
    return high, (value - high.astype(F32)).astype(BF16)


def loop(first, last, body):
    def step(index, carry):
        body(index)
        return carry

    lax.fori_loop(first, last, step, 0)


def kernel(
    x1_h, x2_h, xv_h, go_h, taps_h, short_h, gain_h, sk_h,
    c1h_h, c1l_h, dh_h, dl_h, mh_h, ml_h, nh_h, nl_h, twc_h, tws_h,
    o1_h, o2_h, ov_h, osal_h, osk_h,
    x1, x2, xv, go, short, gain, sk,
    c1h, c1l, dh, dl, mh, ml, nh, nl, twc, tws,
    wrow, wcol, tail_s, tail_r, edge_s, edge_r, hcol,
    gg_s, g_s, act2, actv,
    taps_r, gg_r, g_r,
    y, zh, zl, spec_t, spec_b, spec_a, e, wh, wl,
    gf_s, mix_s, gmix_s, gf_r, mix_r, gmix_r,
    part_s, rs_r, ga1, ga2, gav, sal_s, sal_r, o1, o2, ov, osal, osk,
    load_sem, self_sem, out_sem, send_sem, recv_sem, halo_send, halo_recv, sal_send, sal_recv,
):
    me = lax.axis_index("seq")
    chan = lax.axis_index("chan")
    core = lax.rem(me, 2)
    half = me // 8
    sibling = me + 1 - 2 * core
    following = lax.rem(me + 1, 16)
    previous = lax.rem(me + 15, 16)

    loads = [
        (x1_h, x1), (x2_h, x2), (xv_h, xv), (go_h, go), (short_h, short), (gain_h, gain),
        (c1h_h, c1h), (c1l_h, c1l), (mh_h, mh), (ml_h, ml), (twc_h, twc), (tws_h, tws),
        (nh_h, nh), (nl_h, nl), (dh_h, dh), (dl_h, dl), (sk_h, sk.at[core]),
    ]
    loads = [pltpu.make_async_copy(a, b, load_sem.at[n]) for n, (a, b) in enumerate(loads)]
    for load in loads:
        load.start()

    barrier = pltpu.get_barrier_semaphore()
    loop(1, 16, lambda i: pl.semaphore_signal(
        barrier, inc=1, device_id=(lax.rem(me + i, 16), chan), device_id_type=MESH))
    loop(1, 8, lambda i: pl.semaphore_signal(
        barrier, inc=1, device_id=(me, lax.rem(chan + i, 8)), device_id_type=MESH))

    def block_of(ref):
        return lambda to: ref.at[pl.ds(pl.multiple_of(to * 32, 32), 32)]

    def slot_of(ref):
        return lambda to: ref.at[to]

    def start_send(kind, source, target, first=1, last=16):
        def one(i):
            to = lax.rem(me + i, 16)
            pltpu.make_async_remote_copy(
                src_ref=source(to), dst_ref=target.at[me],
                send_sem=send_sem.at[kind, i], recv_sem=recv_sem.at[kind, i],
                device_id=(to, chan), device_id_type=MESH,
            ).start()

        loop(first, last, one)

    def wait_arrived(kind, source, target):
        def one(i):
            origin = lax.rem(me + 16 - i, 16)
            pltpu.make_async_remote_copy(
                src_ref=source(origin), dst_ref=target.at[origin],
                send_sem=send_sem.at[kind, i], recv_sem=recv_sem.at[kind, i],
                device_id=(origin, chan), device_id_type=MESH,
            ).wait_recv()

        loop(1, 16, one)

    def wait_sent(kind, source, target):
        def one(i):
            to = lax.rem(me + i, 16)
            pltpu.make_async_remote_copy(
                src_ref=source(to), dst_ref=target.at[me],
                send_sem=send_sem.at[kind, i], recv_sem=recv_sem.at[kind, i],
                device_id=(to, chan), device_id_type=MESH,
            ).wait_send()

        loop(1, 16, one)

    def own(kind, source, target):
        return pltpu.make_async_copy(source(me), target.at[me], self_sem.at[kind])

    def neighbour(source, target, n, to):
        return pltpu.make_async_remote_copy(
            src_ref=source, dst_ref=target, send_sem=halo_send.at[n], recv_sem=halo_recv.at[n],
            device_id=(to, chan), device_id_type=MESH)

    for n in range(6):
        loads[n].wait()
    row = lax.broadcasted_iota(jnp.int32, (16, 128), 0)
    lane = lax.broadcasted_iota(jnp.int32, (16, 128), 1)
    tails = jnp.zeros((16, 512), F32)
    for s, ref in enumerate((x1, x2, xv)):
        pick = ((row == 2 * s) & (lane == 126)) | ((row == 2 * s + 1) & (lane == 127))
        tails += dot_nt(pick.astype(F32).astype(BF16), ref[:, 384:512])
    tail_s[...] = tails.astype(BF16)

    pl.semaphore_wait(barrier, 22)
    tail_copy = neighbour(tail_s, tail_r, 0, following)
    tail_copy.start()
    start_send(0, block_of(taps_h), taps_r, 1, 7)
    own(0, block_of(taps_h), taps_r).start()

    wrow[...] = jnp.zeros((128, 512), F32)
    for s in range(3):
        wrow[3 * s : 3 * s + 3, :] = short[s]
    wrow[9:10, :] = gain[...]
    wcol[...] = jnp.transpose(wrow[...])

    tail_copy.wait_recv()
    wrow[0:16, :] = tail_r[...].astype(F32) * (me > 0).astype(F32)
    hcol[...] = jnp.transpose(wrow[...])

    lane32 = lax.broadcasted_iota(jnp.int32, (32, 512), 1)

    def gate(block):
        rows = pl.ds(pl.multiple_of(block * 32, 32), 32)
        weight = wcol[rows, :]
        halo = hcol[rows, :]

        def short_filter(ref, s):
            field = ref[rows, :].astype(F32)
            before, last = halo[:, 2 * s : 2 * s + 1], halo[:, 2 * s + 1 : 2 * s + 2]
            one = jnp.where(lane32 == 0, last, pltpu.roll(field, 1, 1))
            two = jnp.where(lane32 == 0, before, jnp.where(lane32 == 1, last, pltpu.roll(field, 2, 1)))
            return (
                weight[:, 3 * s : 3 * s + 1] * field
                + weight[:, 3 * s + 1 : 3 * s + 2] * one
                + weight[:, 3 * s + 2 : 3 * s + 3] * two
            )

        first = short_filter(x1, 0)
        gg_s[rows, :] = (go[rows, :].astype(F32) * first).astype(BF16)
        second = short_filter(x2, 1)
        value = short_filter(xv, 2)
        act2[rows, :] = second
        actv[rows, :] = value
        g_s[rows, :] = (second * value).astype(BF16)

    loop(0, 16, gate)
    start_send(1, block_of(gg_s), gg_r)
    own(1, block_of(gg_s), gg_r).start()
    start_send(2, block_of(g_s), g_r)
    own(2, block_of(g_s), g_r).start()
    start_send(0, block_of(taps_h), taps_r, 7, 16)
    swap = neighbour(sk_h, sk.at[core], 2, sibling)
    swap.start()

    def first_rows(tile, part, k1):
        return y[tile, pl.ds(pl.multiple_of(part * 256 + k1 * 16, 16), 16), :]

    def store_z(index, re, im):
        for g in range(2):
            rows = pl.ds(pl.multiple_of(index * 32 + g * 16, 16), 16)
            side = slice(g * 128, g * 128 + 128)
            high, low = halves(jnp.concatenate([re[:, side], im[:, side]], axis=1))
            zh[rows, :] = high
            zl[rows, :] = low

    def twist(index, re, im):
        cos, sin = twc[pl.ds(index, 1), :], tws[pl.ds(index, 1), :]
        store_z(index, re * cos + im * sin, im * cos - re * sin)

    def forward(source, spec):
        def stage(tile):
            lanes = pl.ds(pl.multiple_of(tile * 128, 128), 128)
            right = jnp.concatenate(
                [source[:, 0:16, lanes].reshape(256, 128), source[:, 16:32, lanes].reshape(256, 128)],
                axis=1)
            y[tile] = dot(c1h[tile], right) + dot(c1l[tile], right)

        loop(0, 4, stage)

        def butterfly(k1):
            r0, r1, r2, r3 = [first_rows(t, 0, k1) for t in range(4)]
            i0, i1, i2, i3 = [first_rows(t, 1, k1) for t in range(4)]
            ar, ai, br, bi = r0 + r2, i0 + i2, r0 - r2, i0 - i2
            cr, ci, dr, di = r1 + r3, i1 + i3, r1 - r3, i1 - i3
            base = (k1 - 1) * 4
            twist(base, ar + cr, ai + ci)
            twist(base + 1, br + di, bi - dr)
            twist(base + 2, ar - cr, ai - ci)
            twist(base + 3, br - di, bi + dr)

        loop(1, 16, butterfly)
        r0, r1, r2, r3 = [first_rows(t, 0, 0) for t in range(4)]
        none = jnp.zeros_like(r0)
        store_z(60, r0 + r1 + r2 + r3, none)
        twist(61, r0 - r2, r3 - r1)
        twist(62, r0 - r1 + r2 - r3, none)
        r0, r1, r2, r3 = [first_rows(t, 1, 0) for t in range(4)]
        twist(63, r0 + ROOT * (r1 - r3), -r2 - ROOT * (r1 + r3))
        twist(64, r0 - ROOT * (r1 - r3), r2 - ROOT * (r1 + r3))

        def last(chunk):
            rows = pl.ds(pl.multiple_of(chunk * CHUNK, 16), CHUNK)
            spec[rows, :] = dot(zh[rows, :], mh[...]) + dot(zl[rows, :], mh[...]) + dot(zh[rows, :], ml[...])

        loop(0, ROWS // CHUNK, last)

    def inverse(spec_l, spec_r, conj, target):
        sign = -1.0 if conj else 1.0

        def first(chunk):
            rows = pl.ds(pl.multiple_of(chunk * CHUNK, 16), CHUNK)
            lr, li = spec_l[rows, 0:128], spec_l[rows, 128:256] * sign
            rr, ri = spec_r[rows, 0:128], spec_r[rows, 128:256]
            high, low = halves(jnp.concatenate([lr * rr - li * ri, lr * ri + li * rr], axis=1))
            e[rows, :] = dot(high, nh[...]) + dot(low, nh[...]) + dot(high, nl[...])

        loop(0, ROWS // CHUNK, first)

        def untwist(index):
            cos, sin = twc[pl.ds(index, 1), :], tws[pl.ds(index, 1), :]
            top = e[pl.ds(pl.multiple_of(index * 32, 32), 16), :]
            low = e[pl.ds(pl.multiple_of(index * 32 + 16, 16), 16), :]
            re = jnp.concatenate([top[:, 0:128], low[:, 0:128]], axis=1)
            im = jnp.concatenate([top[:, 128:256], low[:, 128:256]], axis=1)
            return re * cos - im * sin, im * cos + re * sin

        def store_w(tile, part, k1, value):
            rows = pl.ds(pl.multiple_of(part * 256 + k1 * 16, 16), 16)
            high, low = halves(value)
            wh[tile, rows, :] = high
            wl[tile, rows, :] = low

        def butterfly(k1):
            base = (k1 - 1) * 4
            (r0, i0), (r1, i1), (r2, i2), (r3, i3) = [untwist(base + q) for q in range(4)]
            ar, ai, br, bi = r0 + r2, i0 + i2, r0 - r2, i0 - i2
            cr, ci, dr, di = r1 + r3, i1 + i3, r1 - r3, i1 - i3
            store_w(0, 0, k1, ar + cr)
            store_w(0, 1, k1, ai + ci)
            store_w(1, 0, k1, br - di)
            store_w(1, 1, k1, bi + dr)
            store_w(2, 0, k1, ar - cr)
            store_w(2, 1, k1, ai - ci)
            store_w(3, 0, k1, br + di)
            store_w(3, 1, k1, bi - dr)

        loop(1, 16, butterfly)
        (r0, _), (r32, i32), (r64, _), (r16, i16), (r48, i48) = [untwist(60 + n) for n in range(5)]
        plus, minus = 0.5 * (r0 + r64), 0.5 * (r0 - r64)
        store_w(0, 0, 0, plus + r32)
        store_w(1, 0, 0, minus - i32)
        store_w(2, 0, 0, plus - r32)
        store_w(3, 0, 0, minus + i32)
        store_w(0, 1, 0, r16 + r48)
        store_w(1, 1, 0, ROOT * (r16 - i16 - r48 - i48))
        store_w(2, 1, 0, i48 - i16)
        store_w(3, 1, 0, ROOT * (r48 - i48 - r16 - i16))

        def last(tile):
            lanes = pl.ds(pl.multiple_of(tile * 128, 128), 128)
            out = dot(dh[tile], wh[tile]) + dot(dh[tile], wl[tile]) + dot(dl[tile], wh[tile])
            out = out.astype(BF16)
            target[:, 0:16, lanes] = out[:, 0:128].reshape(16, 16, 128)
            target[:, 16:32, lanes] = out[:, 128:256].reshape(16, 16, 128)

        loop(0, 4, last)

    for n in range(6, 16):
        loads[n].wait()
    own(1, block_of(gg_s), gg_r).wait()
    wait_arrived(1, block_of(gg_s), gg_r)
    forward(gg_r, spec_b)
    own(2, block_of(g_s), g_r).wait()
    wait_arrived(2, block_of(g_s), g_r)
    forward(g_r, spec_a)
    inverse(spec_a, spec_b, True, gf_s)

    def filter_source(chip):
        return gf_s.at[pl.ds(2 * chip, 2)]

    def filter_copy(chip):
        to = 2 * chip + half
        return pltpu.make_async_remote_copy(
            src_ref=filter_source(chip), dst_ref=gf_r.at[me - 8 * half],
            send_sem=send_sem.at[3, chip], recv_sem=recv_sem.at[3, me - 8 * half],
            device_id=(to, chan), device_id_type=MESH)

    def filter_own():
        return pltpu.make_async_copy(
            filter_source(me // 2), gf_r.at[me - 8 * half], self_sem.at[3])

    def send_filter(n):
        chip = lax.rem(me // 2 + n, 8)

        @pl.when(2 * chip + half != me)
        def _():
            filter_copy(chip).start()

    loop(0, 8, send_filter)

    @pl.when(core == half)
    def _():
        filter_own().start()

    own(0, block_of(taps_h), taps_r).wait()
    wait_arrived(0, block_of(taps_h), taps_r)
    forward(taps_r, spec_t)
    inverse(spec_t, spec_a, False, mix_s)
    start_send(4, slot_of(mix_s), mix_r)
    own(4, slot_of(mix_s), mix_r).start()
    inverse(spec_t, spec_b, True, gmix_s)
    start_send(5, slot_of(gmix_s), gmix_r)
    own(5, slot_of(gmix_s), gmix_r).start()

    loads[16].wait()
    swap_in = neighbour(sk_h, sk.at[1 - core], 2, sibling)
    swap_in.wait_recv()

    @pl.when(core == half)
    def _():
        filter_own().wait()

    def filter_arrived(n):
        origin = 8 * core + n

        @pl.when(origin != me)
        def _():
            pltpu.make_async_remote_copy(
                src_ref=filter_source(0), dst_ref=gf_r.at[n],
                send_sem=send_sem.at[3, 0], recv_sem=recv_sem.at[3, n],
                device_id=(origin, chan), device_id_type=MESH).wait_recv()

    loop(0, 8, filter_arrived)

    def sketch_rows(block):
        rows = pl.ds(pl.multiple_of(block * 256, 256), 256)
        total = dot_nt(sk[0, rows, :], gf_r[:, 0].reshape(256, 512))
        total += dot_nt(sk[1, rows, :], gf_r[:, 1].reshape(256, 512))
        part_s[pl.ds(block * 4, 4)] = total.astype(BF16).reshape(4, 64, 256)

    loop(0, 4, sketch_rows)
    start_send(6, slot_of(part_s), rs_r)
    own(6, slot_of(part_s), rs_r).start()

    own(4, slot_of(mix_s), mix_r).wait()
    wait_arrived(4, slot_of(mix_s), mix_r)
    own(5, slot_of(gmix_s), gmix_r).wait()
    wait_arrived(5, slot_of(gmix_s), gmix_r)

    def activations(block):
        rows = pl.ds(pl.multiple_of(block * 32, 32), 32)
        skip = wcol[rows, 9:10]
        mixed = mix_r[block].astype(F32) + skip * g_s[rows, :].astype(F32)
        ga1[rows, :] = go[rows, :].astype(F32) * mixed
        grad_mix = gmix_r[block].astype(F32) + skip * gg_s[rows, :].astype(F32)
        ga2[rows, :] = grad_mix * actv[rows, :]
        gav[rows, :] = grad_mix * act2[rows, :]

    loop(0, 16, activations)
    edges = jnp.zeros((16, 512), F32)
    for s, ref in enumerate((ga1, ga2, gav)):
        pick = ((row == 2 * s) & (lane == 0)) | ((row == 2 * s + 1) & (lane == 1))
        edges += dot_nt(pick.astype(F32).astype(BF16), ref[:, 0:128].astype(BF16))
    edge_s[...] = edges.astype(BF16)
    edge_copy = neighbour(edge_s, edge_r, 1, previous)
    edge_copy.start()
    edge_copy.wait_recv()
    wrow[0:16, :] = edge_r[...].astype(F32) * (me < 15).astype(F32)
    hcol[...] = jnp.transpose(wrow[...])
    sal_s[...] = jnp.zeros((8, 512), F32)

    def adjoint(block):
        rows = pl.ds(pl.multiple_of(block * 32, 32), 32)
        weight = wcol[rows, :]
        halo = hcol[rows, :]
        total = jnp.zeros((32, 512), F32)
        for s, (grad, stream, out) in enumerate(((ga1, x1, o1), (ga2, x2, o2), (gav, xv, ov))):
            field = grad[rows, :]
            next_one, next_two = halo[:, 2 * s : 2 * s + 1], halo[:, 2 * s + 1 : 2 * s + 2]
            one = jnp.where(lane32 == 511, next_one, pltpu.roll(field, 511, 1))
            two = jnp.where(
                lane32 == 511, next_two, jnp.where(lane32 == 510, next_one, pltpu.roll(field, 510, 1)))
            full = (
                weight[:, 3 * s : 3 * s + 1] * field
                + weight[:, 3 * s + 1 : 3 * s + 2] * one
                + weight[:, 3 * s + 2 : 3 * s + 3] * two
            )
            out[rows, :] = full.astype(BF16)
            total += stream[rows, :].astype(F32) * full
        sal_s[...] += total[0:8] + total[8:16] + total[16:24] + total[24:32]

    loop(0, 16, adjoint)
    outs = [
        pltpu.make_async_copy(a, b, out_sem.at[n])
        for n, (a, b) in enumerate(((o1, o1_h), (o2, o2_h), (ov, ov_h), (osk, osk_h), (osal, osal_h)))
    ]
    for n in range(3):
        outs[n].start()

    def sal_copy(i, to, slot):
        return pltpu.make_async_remote_copy(
            src_ref=sal_s, dst_ref=sal_r.at[slot], send_sem=sal_send.at[i], recv_sem=sal_recv.at[i],
            device_id=(me, to), device_id_type=MESH)

    loop(1, 8, lambda i: sal_copy(i, lax.rem(chan + i, 8), chan).start())
    sal_r[chan] = sal_s[...]

    own(6, slot_of(part_s), rs_r).wait()
    wait_arrived(6, slot_of(part_s), rs_r)
    for side in range(2):
        total = rs_r[side].astype(F32)
        for chip in range(1, 8):
            total += rs_r[2 * chip + side].astype(F32)
        osk[:, side * 256 : side * 256 + 256] = total
    outs[3].start()

    def sal_arrived(i):
        origin = lax.rem(chan + 8 - i, 8)
        sal_copy(i, origin, origin).wait_recv()

    loop(1, 8, sal_arrived)
    total = sal_r[0]
    for n in range(1, 8):
        total += sal_r[n]
    total = jnp.sum(total, axis=0, keepdims=True) * (3.0 * D) ** (-0.5)
    total = jnp.broadcast_to(total, (8, 512))
    osal[...] = pltpu.roll(total, 512 - chan * 64, 1)[:, 0:128]
    outs[4].start()

    tail_copy.wait_send()
    edge_copy.wait_send()
    swap.wait_send()
    wait_sent(0, block_of(taps_h), taps_r)
    wait_sent(1, block_of(gg_s), gg_r)
    wait_sent(2, block_of(g_s), g_r)

    def filter_sent(chip):
        @pl.when(2 * chip + half != me)
        def _():
            filter_copy(chip).wait_send()

    loop(0, 8, filter_sent)
    wait_sent(4, slot_of(mix_s), mix_r)
    wait_sent(5, slot_of(gmix_s), gmix_r)
    wait_sent(6, slot_of(part_s), rs_r)
    loop(1, 8, lambda i: sal_copy(i, lax.rem(chan + i, 8), chan).wait_send())
    for out in outs:
        out.wait()


def on_device(*arrays):
    one, two, value, grad, taps, short, gain, sketch = arrays
    tables = [jnp.asarray(t) for t in host_tables()]
    operands = [one, two, value, grad, taps, short, gain.reshape(1, 512), sketch] + tables

    def vmem(shape, dtype=BF16):
        return pltpu.VMEM(shape, dtype)

    square = (512, 512)
    parts = (16, 32, 512)
    scratch = [
        *[vmem(square) for _ in range(4)], vmem((3, 3, 512), F32), vmem((1, 512), F32), vmem((2, 1024, 512)),
        *[vmem(t.shape, t.dtype) for t in tables],
        vmem((128, 512), F32), vmem((512, 128), F32),
        vmem((16, 512)), vmem((16, 512)), vmem((16, 512)), vmem((16, 512)), vmem((512, 128), F32),
        vmem(square), vmem(square), vmem(square, F32), vmem(square, F32),
        *[vmem(parts) for _ in range(3)],
        vmem((4, 512, 256), F32), vmem((ROWS, 256)), vmem((ROWS, 256)),
        *[vmem((ROWS, 256), F32) for _ in range(4)], vmem((4, 512, 256)), vmem((4, 512, 256)),
        *[vmem(parts) for _ in range(3)], vmem((8, 2, 32, 512)), vmem(parts), vmem(parts),
        vmem((16, 64, 256)), vmem((16, 64, 256)),
        *[vmem(square, F32) for _ in range(3)], vmem((8, 512), F32), vmem((8, 8, 512), F32),
        *[vmem(square) for _ in range(3)], vmem((8, 128), F32), vmem((64, 512), F32),
        pltpu.SemaphoreType.DMA((17,)), pltpu.SemaphoreType.DMA((7,)), pltpu.SemaphoreType.DMA((5,)),
        pltpu.SemaphoreType.DMA((7, 16)), pltpu.SemaphoreType.DMA((7, 16)),
        pltpu.SemaphoreType.DMA((3,)), pltpu.SemaphoreType.DMA((3,)),
        pltpu.SemaphoreType.DMA((8,)), pltpu.SemaphoreType.DMA((8,)),
    ]
    grad_one, grad_two, grad_value, saliency, sketched = pl.pallas_call(
        kernel,
        out_shape=[
            *[jax.ShapeDtypeStruct(square, BF16) for _ in range(3)],
            jax.ShapeDtypeStruct((8, 128), F32),
            jax.ShapeDtypeStruct((64, 512), F32),
        ],
        in_specs=[pl.BlockSpec(memory_space=pl.ANY) for _ in operands],
        out_specs=[pl.BlockSpec(memory_space=pl.ANY) for _ in range(5)],
        scratch_shapes=scratch,
        compiler_params=pltpu.CompilerParams(
            collective_id=0, has_side_effects=True, vmem_limit_bytes=56 * 1024 * 1024),
    )(*operands)
    return grad_one, grad_two, grad_value, saliency[0, :64], sketched


def solution(mesh):
    return jax.shard_map(
        on_device,
        mesh=mesh,
        in_specs=(
            P("chan", "seq"),
            P("chan", "seq"),
            P("chan", "seq"),
            P("chan", "seq"),
            P("chan", "seq"),
            P(None, None, "chan"),
            P("chan"),
            P(None, "seq"),
        ),
        out_specs=(
            P("chan", "seq"),
            P("chan", "seq"),
            P("chan", "seq"),
            P(("seq", "chan")),
            P("seq", "chan"),
        ),
        check_vma=False,
    )
```

time: 305 us -> 82.5 us (0.27); the launches traced: 301 us -> 82.2 us
  blocking collectives: 84.5 us -> 0 us
  Pallas kernels: 0 us -> 75.6 us
  matrix products: 73.3 us -> 0 us
  waiting for transfers between devices: 55.9 us -> 0 us
  starting transfers between devices: 41.1 us -> 0 us
  local copies, waits for them, and re-layouts: 22.3 us -> 6.03 us
  between operations: 14.8 us -> 0.65 us
  other arithmetic: 8.73 us -> 0 us
    pallas_call x0 -> x1, Pallas kernels: none -> 75.6 us  [on_device(): pl.pallas_call(kernel, out_shape=[*[jax.ShapeDtypeStruct(square, BF16) fo...]
    dot_general x37 -> x0, matrix products: 73.3 us -> none  [the longest x36 62.5 us: product(): return jnp.einsum(form, left, right, precision=lax.Precision.HIGH)]
    unnamed x1 -> x0, blocking collectives: 67.5 us -> none
    all_to_all x8 -> x0, waiting for transfers between devices: 55.2 us -> none  [the longest x1 13.9 us: on_device(): lax.all_to_all(stream_value, 'seq', split_axis=0, concat_axis=1, tiled=True)]
    all_to_all x8 -> x0, starting transfers between devices: 41.1 us -> none  [the longest x1 5.78 us: on_device(): lax.all_to_all(whole_sketch, 'seq', split_axis=0, concat_axis=1, tiled=True)]
    all_to_all x1 -> x0, blocking collectives: 17 us -> none  [on_device(): lax.all_to_all(stream_one, 'seq', split_axis=0, concat_axis=1, tiled=True)]
    all_to_all x7 -> x0, local copies, waits for them, and re-layouts: 5.38 us -> none  [the longest x1 2.13 us: on_device(): lax.all_to_all(long_taps, 'seq', split_axis=0, concat_axis=1, tiled=True)]
    slice x6 -> x0, local copies, waits for them, and re-layouts: 5.06 us -> none  [advance(): return jnp.pad(field[:, steps:], ((0, 0), (0, steps)))]
  transfers between devices with their start and end apart: 9 -> 0, of which waited for: 6 -> 0; matrix products, arithmetic and copies ran while one was open for 32% -> 0% of each run, Pallas kernels for 0% -> 0%
where the time goes in v1:
time: 82.5 us; the launch traced here: 82.2 us
  Pallas kernels  75.6 us (92%)
  local copies, waits for them, and re-layouts  6.03 us (7%)
    pallas_call x1, Pallas kernels, on_device(): pl.pallas_call(kernel, out_shape=[*[jax.ShapeDtypeStruct(square, BF16) fo...  75.6 us
    unnamed x10, local copies, waits for them, and re-layouts  4.84 us

profile of v1, /device:TPU:1, one launch (start us, length us, event | category | flops | bytes accessed | tf_op | source)
XLA Modules:
  0.0 82.2 jit_solution(16252175461590412038)
XLA Ops:
  0.6 75.6 %shard_map.209 = (bf16[512,512]{1,0:T(8,128)(2,1)}, bf16[512,512]{1,0:T(8,128)(2,1)}, bf16[512,512]{1,0:T(8,128)(2,1)}, f32[8,128]{1,0:T(8,128)}, f32[64,512]{1,0:T(8,128)}) custom-call(bf16[512,512]{1,0:T(8,128)(2,1)} %x1_h.1, bf16[512,512]{1,0:T(8,128)(2,1)} %x2_h.1, bf16[512,512]{1,0:T(8,128)(2,1)} %xv_h.1, bf16[512,512]{1,0:T(8,128)(2,1)} %go_h.1, ...), custom_call_target="tpu_custom_call" | custom-call | tf_op jit(solution)/shard_map/pallas_call | solution.py:547
  76.2 1.2 %slice_bitcast_fusion = f32[64]{0:T(128)} fusion(f32[8,128]{1,0:T(8,128)} %get-tuple-element.13), kind=kLoop, calls=%fused_computation | loop fusion | bytes 512 | tf_op jit(solution)/shard_map/squeeze | solution.py:560
  77.4 0.0 copy-start.1
  77.4 1.9 %copy.27 = bf16[512,512]{1,0:T(8,128)(2,1)} copy(bf16[512,512]{1,0:T(8,128)(2,1)} %get-tuple-element.20) | data formatting | bytes 1048576
  79.3 0.0 copy-done.1
  79.3 0.0 copy-start
  79.3 0.8 copy.28
  80.1 0.4 copy-done
  80.5 0.0 copy-start.2
  80.5 0.8 copy.29
  81.3 0.2 copy-done.2
  81.6 0.7 copy.30
Async XLA Ops:
  77.4 1.9 %copy-start.1 = (bf16[512,512]{1,0:T(8,128)(2,1)S(1)}, bf16[512,512]{1,0:T(8,128)(2,1)}, u32[]{:S(2)}) copy-start(bf16[512,512]{1,0:T(8,128)(2,1)} %get-tuple-element.21) | copy-start | bytes 1572868
  79.3 1.2 %copy-start = (bf16[512,512]{1,0:T(8,128)(2,1)S(1)}, bf16[512,512]{1,0:T(8,128)(2,1)}, u32[]{:S(2)}) copy-start(bf16[512,512]{1,0:T(8,128)(2,1)} %get-tuple-element.22) | copy-start | bytes 1572868
  80.5 1.0 %copy-start.2 = (f32[64,512]{1,0:T(8,128)S(1)}, f32[64,512]{1,0:T(8,128)}, u32[]{:S(2)}) copy-start(f32[64,512]{1,0:T(8,128)} %get-tuple-element.24) | copy-start | bytes 393220

commit v2 on v1

v2 whole, which is shorter than its diff:
```python
import functools
import math

import jax
import jax.numpy as jnp
import numpy as np
from jax import lax
from jax.experimental import pallas as pl
from jax.experimental.pallas import tpu as pltpu
from jax.sharding import PartitionSpec as P

D = 4096
MESH = pl.DeviceIdType.MESH
F32 = jnp.float32
BF16 = jnp.bfloat16
ROOT = math.sqrt(0.5)
FREQS = [k1 + 32 * q for k1 in range(1, 16) for q in range(4)] + [0, 32, 64, 16, 48]
ROWS = 32 * len(FREQS)


def split_host(table):
    high = table.astype(jnp.bfloat16)
    low = (table - high.astype(np.float64)).astype(jnp.bfloat16)
    return high, low


def host_tables():
    shard = np.arange(16)
    k1 = np.arange(16)
    first = np.zeros((4, 32, 16))
    for tile in range(4):
        angle = 2 * np.pi * np.outer(k1, 4 * shard + tile) / 128
        first[tile, :16] = np.cos(angle)
        first[tile, 16:] = -np.sin(angle)
        first[tile, 16] = (-1.0) ** shard
    eye = np.eye(16)
    wide = np.einsum("tks,cd->tkcsd", first, eye).reshape(4, 512, 256)
    back = np.einsum("tks,cd->tsckd", first, eye).reshape(4, 256, 512) * (2.0 / 16384)
    lane = np.arange(128)
    angle = 2 * np.pi * np.outer(lane, lane) / 128
    cos, sin = np.cos(angle), np.sin(angle)
    inner = np.block([[cos, -sin], [sin, cos]])
    inner_back = np.block([[cos, sin], [-sin, cos]])
    twist = 2 * np.pi * np.outer(np.array(FREQS + [0] * 7), lane) / 16384
    twist = np.concatenate([twist, twist], axis=1)
    return (
        *split_host(wide),
        *split_host(back),
        *split_host(inner),
        *split_host(inner_back),
        np.cos(twist).astype(np.float32),
        np.sin(twist).astype(np.float32),
    )


def dot(left, right):
    return jnp.dot(left, right, preferred_element_type=F32)


def dot_nt(left, right):
    return lax.dot_general(left, right, (((1,), (1,)), ((), ())), preferred_element_type=F32)


def halves(value):
    high = value.astype(BF16)
    return high, (value - high.astype(F32)).astype(BF16)


def loop(first, last, body):
    def step(index, carry):
        body(index)
        return carry

    lax.fori_loop(first, last, step, 0)


def kernel(
    x1_h, x2_h, xv_h, go_h, taps_h, short_h, gain_h, sk_h,
    c1h_h, c1l_h, dh_h, dl_h, mh_h, ml_h, nh_h, nl_h, twc_h, tws_h,
    o1_h, o2_h, ov_h, osal_h, osk_h,
    x1, x2, xv, go, short, gain, sk,
    c1h, c1l, dh, dl, mh, ml, nh, nl, twc, tws,
    wrow, wcol, tail_s, tail_r, edge_s, edge_r, hcol,
    act2, actv,
    pair_s, pair_r, taps_r,
    y, zh, zl, spec_t, spec_p, e, wh, wl,
    gf_s, gf_r, mm_s, mm_r,
    part_s, rs_r, ga1, ga2, gav, sal_s, sal_r, o1, o2, ov, osal, osk,
    load_sem, out_sem, send_sem, recv_sem, halo_send, halo_recv, sal_send, sal_recv,
):
    me = lax.axis_index("seq")
    chan = lax.axis_index("chan")
    core = lax.rem(me, 2)
    half = me // 8
    sibling = me + 1 - 2 * core
    following = lax.rem(me + 1, 16)
    previous = lax.rem(me + 15, 16)

    loads = [
        (x1_h, x1), (x2_h, x2), (xv_h, xv), (go_h, go), (short_h, short), (gain_h, gain),
        (c1h_h, c1h), (c1l_h, c1l), (mh_h, mh), (ml_h, ml), (twc_h, twc), (tws_h, tws),
        (nh_h, nh), (nl_h, nl), (dh_h, dh), (dl_h, dl), (sk_h, sk.at[core]),
    ]
    loads = [pltpu.make_async_copy(a, b, load_sem.at[n]) for n, (a, b) in enumerate(loads)]
    for load in loads:
        load.start()

    barrier = pltpu.get_barrier_semaphore()
    loop(1, 16, lambda i: pl.semaphore_signal(
        barrier, inc=1, device_id=(lax.rem(me + i, 16), chan), device_id_type=MESH))
    loop(1, 8, lambda i: pl.semaphore_signal(
        barrier, inc=1, device_id=(me, lax.rem(chan + i, 8)), device_id_type=MESH))

    def block_of(ref):
        return lambda to: ref.at[pl.ds(pl.multiple_of(to * 32, 32), 32)]

    def slot_of(ref):
        return lambda to: ref.at[to]

    def send_all(kind, source, target):
        def one(i):
            to = lax.rem(me + i, 16)
            pltpu.make_async_remote_copy(
                src_ref=source(to), dst_ref=target.at[me],
                send_sem=send_sem.at[kind], recv_sem=recv_sem.at[kind],
                device_id=(to, chan), device_id_type=MESH,
            ).start()

        loop(1, 16, one)
        pltpu.make_async_copy(source(me), target.at[me], recv_sem.at[kind]).start()

    def wait_bytes(ref, sem):
        pltpu.make_async_copy(ref, ref, sem).wait()

    def neighbour(source, target, n, to):
        return pltpu.make_async_remote_copy(
            src_ref=source, dst_ref=target, send_sem=halo_send.at[n], recv_sem=halo_recv.at[n],
            device_id=(to, chan), device_id_type=MESH)

    for n in range(6):
        loads[n].wait()
    row = lax.broadcasted_iota(jnp.int32, (16, 128), 0)
    lane = lax.broadcasted_iota(jnp.int32, (16, 128), 1)
    tails = jnp.zeros((16, 512), F32)
    for s, ref in enumerate((x1, x2, xv)):
        pick = ((row == 2 * s) & (lane == 126)) | ((row == 2 * s + 1) & (lane == 127))
        tails += dot_nt(pick.astype(F32).astype(BF16), ref[:, 384:512])
    tail_s[...] = tails.astype(BF16)

    pl.semaphore_wait(barrier, 22)
    tail_copy = neighbour(tail_s, tail_r, 0, following)
    tail_copy.start()
    send_all(0, block_of(taps_h), taps_r)

    wrow[...] = jnp.zeros((128, 512), F32)
    for s in range(3):
        wrow[3 * s : 3 * s + 3, :] = short[s]
    wrow[9:10, :] = gain[...]
    wcol[...] = jnp.transpose(wrow[...])

    tail_copy.wait_recv()
    wrow[0:16, :] = tail_r[...].astype(F32) * (me > 0).astype(F32)
    hcol[...] = jnp.transpose(wrow[...])

    lane16 = lax.broadcasted_iota(jnp.int32, (16, 512), 1)

    def rows_of(block, h):
        return pl.ds(pl.multiple_of(block * 32 + h * 16, 16), 16)

    def gate(h):
        def body(block):
            rows = rows_of(block, h)
            weight = wcol[rows, :]
            halo = hcol[rows, :]

            def short_filter(ref, s):
                field = ref[rows, :].astype(F32)
                before, last = halo[:, 2 * s : 2 * s + 1], halo[:, 2 * s + 1 : 2 * s + 2]
                one = jnp.where(lane16 == 0, last, pltpu.roll(field, 1, 1))
                two = jnp.where(lane16 == 0, before, jnp.where(lane16 == 1, last, pltpu.roll(field, 2, 1)))
                return (
                    weight[:, 3 * s : 3 * s + 1] * field
                    + weight[:, 3 * s + 1 : 3 * s + 2] * one
                    + weight[:, 3 * s + 2 : 3 * s + 3] * two
                )

            first = short_filter(x1, 0)
            pair_s[h, block, 0] = (go[rows, :].astype(F32) * first).astype(BF16)
            second = short_filter(x2, 1)
            value = short_filter(xv, 2)
            act2[rows, :] = second
            actv[rows, :] = value
            pair_s[h, block, 1] = (second * value).astype(BF16)

        loop(0, 16, body)

    for h in range(2):
        gate(h)
        send_all(1 + h, slot_of(pair_s.at[h]), pair_r.at[h])
    swap = neighbour(sk_h, sk.at[core], 2, sibling)
    swap.start()

    def first_rows(tile, part, k1):
        return y[tile, pl.ds(pl.multiple_of(part * 256 + k1 * 16, 16), 16), :]

    def store_z(index, re, im):
        for g in range(2):
            rows = pl.ds(pl.multiple_of(index * 32 + g * 16, 16), 16)
            side = slice(g * 128, g * 128 + 128)
            high, low = halves(jnp.concatenate([re[:, side], im[:, side]], axis=1))
            zh[rows, :] = high
            zl[rows, :] = low

    def twist(index, re, im):
        cos, sin = twc[pl.ds(index, 1), :], tws[pl.ds(index, 1), :]
        store_z(index, re * cos + im * sin, im * cos - re * sin)

    def forward(source, spec):
        def stage(tile):
            lanes = pl.ds(pl.multiple_of(tile * 128, 128), 128)
            right = jnp.concatenate([source(g, lanes).reshape(256, 128) for g in range(2)], axis=1)
            y[tile] = dot(c1h[tile], right) + dot(c1l[tile], right)

        loop(0, 4, stage)

        def butterfly(k1):
            r0, r1, r2, r3 = [first_rows(t, 0, k1) for t in range(4)]
            i0, i1, i2, i3 = [first_rows(t, 1, k1) for t in range(4)]
            ar, ai, br, bi = r0 + r2, i0 + i2, r0 - r2, i0 - i2
            cr, ci, dr, di = r1 + r3, i1 + i3, r1 - r3, i1 - i3
            base = (k1 - 1) * 4
            twist(base, ar + cr, ai + ci)
            twist(base + 1, br + di, bi - dr)
            twist(base + 2, ar - cr, ai - ci)
            twist(base + 3, br - di, bi + dr)

        loop(1, 16, butterfly)
        r0, r1, r2, r3 = [first_rows(t, 0, 0) for t in range(4)]
        none = jnp.zeros_like(r0)
        store_z(60, r0 + r1 + r2 + r3, none)
        twist(61, r0 - r2, r3 - r1)
        twist(62, r0 - r1 + r2 - r3, none)
        r0, r1, r2, r3 = [first_rows(t, 1, 0) for t in range(4)]
        twist(63, r0 + ROOT * (r1 - r3), -r2 - ROOT * (r1 + r3))
        twist(64, r0 - ROOT * (r1 - r3), r2 - ROOT * (r1 + r3))

        def last(chunk):
            rows = pl.ds(pl.multiple_of(chunk * 416, 16), 416)
            out = dot(zh[rows, :], mh[...]) + dot(zl[rows, :], mh[...]) + dot(zh[rows, :], ml[...])
            spec[pl.ds(chunk * 13, 13)] = out.reshape(13, 32, 256)

        loop(0, 5, last)

    def times(left, right, sign):
        lr, li = left[..., 0:128], left[..., 128:256] * sign
        rr, ri = right[..., 0:128], right[..., 128:256]
        return jnp.concatenate([lr * rr - li * ri, lr * ri + li * rr], axis=2)

    def inverse(product, count, store):
        size = 16 * count
        wide = 128 * count

        def first(chunk):
            high, low = halves(product(pl.ds(chunk * 13, 13)).reshape(13 * size, 256))
            rows = pl.ds(pl.multiple_of(chunk * 13 * size, 16), 13 * size)
            e[rows, :] = dot(high, nh[...]) + dot(low, nh[...]) + dot(high, nl[...])

        loop(0, 5, first)

        def untwist(index):
            cos, sin = twc[pl.ds(index, 1), :][:, 0:wide], tws[pl.ds(index, 1), :][:, 0:wide]
            parts = [e[pl.ds(pl.multiple_of(index * size + 16 * g, 16), 16), :] for g in range(count)]
            re = jnp.concatenate([p[:, 0:128] for p in parts], axis=1)
            im = jnp.concatenate([p[:, 128:256] for p in parts], axis=1)
            return re * cos - im * sin, im * cos + re * sin

        def store_w(tile, part, k1, value):
            rows = pl.ds(pl.multiple_of(part * 256 + k1 * 16, 16), 16)
            high, low = halves(value)
            wh[tile, rows, 0:wide] = high
            wl[tile, rows, 0:wide] = low

        def butterfly(k1):
            base = (k1 - 1) * 4
            (r0, i0), (r1, i1), (r2, i2), (r3, i3) = [untwist(base + q) for q in range(4)]
            ar, ai, br, bi = r0 + r2, i0 + i2, r0 - r2, i0 - i2
            cr, ci, dr, di = r1 + r3, i1 + i3, r1 - r3, i1 - i3
            store_w(0, 0, k1, ar + cr)
            store_w(0, 1, k1, ai + ci)
            store_w(1, 0, k1, br - di)
            store_w(1, 1, k1, bi + dr)
            store_w(2, 0, k1, ar - cr)
            store_w(2, 1, k1, ai - ci)
            store_w(3, 0, k1, br + di)
            store_w(3, 1, k1, bi - dr)

        loop(1, 16, butterfly)
        (r0, _), (r32, i32), (r64, _), (r16, i16), (r48, i48) = [untwist(60 + n) for n in range(5)]
        plus, minus = 0.5 * (r0 + r64), 0.5 * (r0 - r64)
        store_w(0, 0, 0, plus + r32)
        store_w(1, 0, 0, minus - i32)
        store_w(2, 0, 0, plus - r32)
        store_w(3, 0, 0, minus + i32)
        store_w(0, 1, 0, r16 + r48)
        store_w(1, 1, 0, ROOT * (r16 - i16 - r48 - i48))
        store_w(2, 1, 0, i48 - i16)
        store_w(3, 1, 0, ROOT * (r48 - i48 - r16 - i16))

        def last(tile):
            lanes = pl.ds(pl.multiple_of(tile * 128, 128), 128)
            high, low = wh[tile, :, 0:wide], wl[tile, :, 0:wide]
            out = (dot(dh[tile], high) + dot(dh[tile], low) + dot(dl[tile], high)).astype(BF16)
            for g in range(count):
                store(g, lanes, out[:, g * 128 : g * 128 + 128].reshape(16, 16, 128))

        loop(0, 4, last)

    def filter_copy(h, chip):
        return pltpu.make_async_remote_copy(
            src_ref=gf_s.at[h, pl.ds(2 * chip, 2)], dst_ref=gf_r.at[me - 8 * half, h],
            send_sem=send_sem.at[3 + h], recv_sem=recv_sem.at[3 + h],
            device_id=(2 * chip + half, chan), device_id_type=MESH)

    def filter_out(h):
        def product(index):
            return times(spec_p[h, index, 16:32, :], spec_p[h, index, 0:16, :], -1.0)

        def store(g, lanes, value):
            gf_s[h, :, :, lanes] = value

        inverse(product, 1, store)

        def one(n):
            chip = lax.rem(me // 2 + n, 8)

            @pl.when(2 * chip + half != me)
            def _():
                filter_copy(h, chip).start()

        loop(0, 8, one)

        @pl.when(core == half)
        def _():
            pltpu.make_async_copy(
                gf_s.at[h, pl.ds(2 * (me // 2), 2)], gf_r.at[me - 8 * half, h], recv_sem.at[3 + h]).start()

    def mixes_out(h):
        def product(index):
            taps = spec_t[index, h * 16 : h * 16 + 16, :]
            return jnp.concatenate(
                [times(taps, spec_p[h, index, 16:32, :], 1.0), times(taps, spec_p[h, index, 0:16, :], -1.0)],
                axis=1)

        def store(g, lanes, value):
            mm_s[h, :, g, :, lanes] = value

        inverse(product, 2, store)
        send_all(5 + h, slot_of(mm_s.at[h]), mm_r.at[h])

    for n in range(6, 16):
        loads[n].wait()
    wait_bytes(taps_r, recv_sem.at[0])
    forward(lambda g, lanes: taps_r[:, g * 16 : g * 16 + 16, lanes], spec_t)
    for h in range(2):
        wait_bytes(pair_r.at[h], recv_sem.at[1 + h])
        forward(lambda g, lanes: pair_r[h, :, g, :, lanes], spec_p.at[h])
        filter_out(h)
        mixes_out(h)

    def activations(h):
        wait_bytes(mm_r.at[h], recv_sem.at[5 + h])

        def body(block):
            rows = rows_of(block, h)
            skip = wcol[rows, 9:10]
            mixed = mm_r[h, block, 0].astype(F32) + skip * pair_s[h, block, 1].astype(F32)
            ga1[rows, :] = go[rows, :].astype(F32) * mixed
            grad_mix = mm_r[h, block, 1].astype(F32) + skip * pair_s[h, block, 0].astype(F32)
            ga2[rows, :] = grad_mix * actv[rows, :]
            gav[rows, :] = grad_mix * act2[rows, :]

        loop(0, 16, body)

    loads[16].wait()
    swap_in = neighbour(sk_h, sk.at[1 - core], 2, sibling)
    swap_in.wait_recv()
    for h in range(2):
        wait_bytes(gf_s.at[h], recv_sem.at[3 + h])

    def sketch_rows(block):
        rows = pl.ds(pl.multiple_of(block * 256, 256), 256)
        total = dot_nt(sk[0, rows, :], gf_r[:, :, 0].reshape(256, 512))
        total += dot_nt(sk[1, rows, :], gf_r[:, :, 1].reshape(256, 512))
        part_s[pl.ds(block * 4, 4)] = total.astype(BF16).reshape(4, 64, 256)

    loop(0, 4, sketch_rows)
    send_all(7, slot_of(part_s), rs_r)

    activations(0)
    activations(1)
    edges = jnp.zeros((16, 512), F32)
    for s, ref in enumerate((ga1, ga2, gav)):
        pick = ((row == 2 * s) & (lane == 0)) | ((row == 2 * s + 1) & (lane == 1))
        edges += dot_nt(pick.astype(F32).astype(BF16), ref[:, 0:128].astype(BF16))
    edge_s[...] = edges.astype(BF16)
    edge_copy = neighbour(edge_s, edge_r, 1, previous)
    edge_copy.start()
    edge_copy.wait_recv()
    wrow[0:16, :] = edge_r[...].astype(F32) * (me < 15).astype(F32)
    hcol[...] = jnp.transpose(wrow[...])
    sal_s[...] = jnp.zeros((8, 512), F32)

    def adjoint(block):
        rows = pl.ds(pl.multiple_of(block * 16, 16), 16)
        weight = wcol[rows, :]
        halo = hcol[rows, :]
        total = jnp.zeros((16, 512), F32)
        for s, (grad, stream, out) in enumerate(((ga1, x1, o1), (ga2, x2, o2), (gav, xv, ov))):
            field = grad[rows, :]
            next_one, next_two = halo[:, 2 * s : 2 * s + 1], halo[:, 2 * s + 1 : 2 * s + 2]
            one = jnp.where(lane16 == 511, next_one, pltpu.roll(field, 511, 1))
            two = jnp.where(
                lane16 == 511, next_two, jnp.where(lane16 == 510, next_one, pltpu.roll(field, 510, 1)))
            full = (
                weight[:, 3 * s : 3 * s + 1] * field
                + weight[:, 3 * s + 1 : 3 * s + 2] * one
                + weight[:, 3 * s + 2 : 3 * s + 3] * two
            )
            out[rows, :] = full.astype(BF16)
            total += stream[rows, :].astype(F32) * full
        sal_s[...] += total[0:8] + total[8:16]

    loop(0, 32, adjoint)
    outs = [
        pltpu.make_async_copy(a, b, out_sem.at[n])
        for n, (a, b) in enumerate(((o1, o1_h), (o2, o2_h), (ov, ov_h), (osk, osk_h), (osal, osal_h)))
    ]
    for n in range(3):
        outs[n].start()

    def sal_send_to(i):
        pltpu.make_async_remote_copy(
            src_ref=sal_s, dst_ref=sal_r.at[chan], send_sem=sal_send.at[0], recv_sem=sal_recv.at[0],
            device_id=(me, lax.rem(chan + i, 8)), device_id_type=MESH).start()

    loop(1, 8, sal_send_to)
    pltpu.make_async_copy(sal_s, sal_r.at[chan], sal_recv.at[0]).start()

    wait_bytes(rs_r, recv_sem.at[7])
    for side in range(2):
        total = rs_r[side].astype(F32)
        for chip in range(1, 8):
            total += rs_r[2 * chip + side].astype(F32)
        osk[:, side * 256 : side * 256 + 256] = total
    outs[3].start()

    wait_bytes(sal_r, sal_recv.at[0])
    total = sal_r[0]
    for n in range(1, 8):
        total += sal_r[n]
    total = jnp.sum(total, axis=0, keepdims=True) * (3.0 * D) ** (-0.5)
    total = jnp.broadcast_to(total, (8, 512))
    osal[...] = pltpu.roll(total, 512 - chan * 64, 1)[:, 0:128]
    outs[4].start()

    tail_copy.wait_send()
    edge_copy.wait_send()
    swap.wait_send()
    wait_bytes(taps_r.at[pl.ds(0, 15)], send_sem.at[0])
    for h in range(2):
        wait_bytes(pair_s.at[h, pl.ds(0, 15)], send_sem.at[1 + h])
        wait_bytes(mm_s.at[h, pl.ds(0, 15)], send_sem.at[5 + h])
        wait_bytes(gf_s.at[h, pl.ds(0, 14)], send_sem.at[3 + h])

        @pl.when(core != half)
        def _():
            wait_bytes(gf_s.at[h, pl.ds(14, 2)], send_sem.at[3 + h])

    wait_bytes(part_s.at[pl.ds(0, 15)], send_sem.at[7])
    wait_bytes(sal_r.at[pl.ds(0, 7)], sal_send.at[0])
    for out in outs:
        out.wait()


def on_device(*arrays):
    one, two, value, grad, taps, short, gain, sketch = arrays
    tables = [jnp.asarray(t) for t in host_tables()]
    operands = [one, two, value, grad, taps, short, gain.reshape(1, 512), sketch] + tables

    def vmem(shape, dtype=BF16):
        return pltpu.VMEM(shape, dtype)

    square = (512, 512)
    parts = (2, 16, 2, 16, 512)
    scratch = [
        *[vmem(square) for _ in range(4)], vmem((3, 3, 512), F32), vmem((1, 512), F32), vmem((2, 1024, 512)),
        *[vmem(t.shape, t.dtype) for t in tables],
        vmem((128, 512), F32), vmem((512, 128), F32),
        vmem((16, 512)), vmem((16, 512)), vmem((16, 512)), vmem((16, 512)), vmem((512, 128), F32),
        vmem(square, F32), vmem(square, F32),
        vmem(parts), vmem(parts), vmem((16, 32, 512)),
        vmem((4, 512, 256), F32), vmem((ROWS, 256)), vmem((ROWS, 256)),
        vmem((65, 32, 256), F32), vmem((2, 65, 32, 256), F32), vmem((ROWS, 256), F32),
        vmem((4, 512, 256)), vmem((4, 512, 256)),
        vmem((2, 16, 16, 512)), vmem((8, 2, 2, 16, 512)), vmem(parts), vmem(parts),
        vmem((16, 64, 256)), vmem((16, 64, 256)),
        *[vmem(square, F32) for _ in range(3)], vmem((8, 512), F32), vmem((8, 8, 512), F32),
        *[vmem(square) for _ in range(3)], vmem((8, 128), F32), vmem((64, 512), F32),
        pltpu.SemaphoreType.DMA((17,)), pltpu.SemaphoreType.DMA((5,)),
        pltpu.SemaphoreType.DMA((8,)), pltpu.SemaphoreType.DMA((8,)),
        pltpu.SemaphoreType.DMA((3,)), pltpu.SemaphoreType.DMA((3,)),
        pltpu.SemaphoreType.DMA((1,)), pltpu.SemaphoreType.DMA((1,)),
    ]
    grad_one, grad_two, grad_value, saliency, sketched = pl.pallas_call(
        kernel,
        out_shape=[
            *[jax.ShapeDtypeStruct(square, BF16) for _ in range(3)],
            jax.ShapeDtypeStruct((8, 128), F32),
            jax.ShapeDtypeStruct((64, 512), F32),
        ],
        in_specs=[pl.BlockSpec(memory_space=pl.ANY) for _ in operands],
        out_specs=[pl.BlockSpec(memory_space=pl.ANY) for _ in range(5)],
        scratch_shapes=scratch,
        compiler_params=pltpu.CompilerParams(
            collective_id=0, has_side_effects=True, vmem_limit_bytes=56 * 1024 * 1024),
    )(*operands)
    return grad_one, grad_two, grad_value, saliency[0, :64], sketched


def solution(mesh):
    return jax.shard_map(
        on_device,
        mesh=mesh,
        in_specs=(
            P("chan", "seq"),
            P("chan", "seq"),
            P("chan", "seq"),
            P("chan", "seq"),
            P("chan", "seq"),
            P(None, None, "chan"),
            P("chan"),
            P(None, "seq"),
        ),
        out_specs=(
            P("chan", "seq"),
            P("chan", "seq"),
            P("chan", "seq"),
            P(("seq", "chan")),
            P("seq", "chan"),
        ),
        check_vma=False,
    )
```

time: 82.5 us -> 77.8 us (0.943)
  Pallas kernels: 75.6 us -> 70.9 us
    pallas_call x1, Pallas kernels: 75.6 us -> 70.9 us  [on_device(): pl.pallas_call(kernel, out_shape=[*[jax.ShapeDtypeStruct(square, BF16) fo...]
where the time goes in v2:
time: 77.8 us; the launch traced here: 77.5 us
  Pallas kernels  70.9 us (91%)
  local copies, waits for them, and re-layouts  6.03 us (8%)
    pallas_call x1, Pallas kernels, on_device(): pl.pallas_call(kernel, out_shape=[*[jax.ShapeDtypeStruct(square, BF16) fo...  70.9 us
    unnamed x10, local copies, waits for them, and re-layouts  4.84 us

profile of v2, /device:TPU:1, one launch (start us, length us, event | category | flops | bytes accessed | tf_op | source)
XLA Modules:
  0.0 77.5 jit_solution(10956701560160404581)
XLA Ops:
  0.6 70.9 %shard_map.209 = (bf16[512,512]{1,0:T(8,128)(2,1)}, bf16[512,512]{1,0:T(8,128)(2,1)}, bf16[512,512]{1,0:T(8,128)(2,1)}, f32[8,128]{1,0:T(8,128)}, f32[64,512]{1,0:T(8,128)}) custom-call(bf16[512,512]{1,0:T(8,128)(2,1)} %x1_h.1, bf16[512,512]{1,0:T(8,128)(2,1)} %x2_h.1, bf16[512,512]{1,0:T(8,128)(2,1)} %xv_h.1, bf16[512,512]{1,0:T(8,128)(2,1)} %go_h.1, ...), custom_call_target="tpu_custom_call" | custom-call | tf_op jit(solution)/shard_map/pallas_call | solution.py:514
  71.5 1.2 %slice_bitcast_fusion = f32[64]{0:T(128)} fusion(f32[8,128]{1,0:T(8,128)} %get-tuple-element.13), kind=kLoop, calls=%fused_computation | loop fusion | bytes 512 | tf_op jit(solution)/shard_map/squeeze | solution.py:527
  72.7 0.0 copy-start.1
  72.7 1.9 %copy.27 = bf16[512,512]{1,0:T(8,128)(2,1)} copy(bf16[512,512]{1,0:T(8,128)(2,1)} %get-tuple-element.20) | data formatting | bytes 1048576
  74.6 0.0 copy-done.1
  74.6 0.0 copy-start
  74.6 0.8 %copy.28 = bf16[512,512]{1,0:T(8,128)(2,1)} copy(bf16[512,512]{1,0:T(8,128)(2,1)S(1)} %copy-done.1) | data formatting | bytes 1048576
  75.4 0.4 copy-done
  75.9 0.0 copy-start.2
  75.9 0.8 %copy.29 = bf16[512,512]{1,0:T(8,128)(2,1)} copy(bf16[512,512]{1,0:T(8,128)(2,1)S(1)} %copy-done) | data formatting | bytes 1048576
  76.7 0.2 copy-done.2
  76.9 0.7 copy.30
Async XLA Ops:
  72.7 1.9 %copy-start.1 = (bf16[512,512]{1,0:T(8,128)(2,1)S(1)}, bf16[512,512]{1,0:T(8,128)(2,1)}, u32[]{:S(2)}) copy-start(bf16[512,512]{1,0:T(8,128)(2,1)} %get-tuple-element.21) | copy-start | bytes 1572868
  74.6 1.2 %copy-start = (bf16[512,512]{1,0:T(8,128)(2,1)S(1)}, bf16[512,512]{1,0:T(8,128)(2,1)}, u32[]{:S(2)}) copy-start(bf16[512,512]{1,0:T(8,128)(2,1)} %get-tuple-element.22) | copy-start | bytes 1572868
  75.9 1.0 %copy-start.2 = (f32[64,512]{1,0:T(8,128)S(1)}, f32[64,512]{1,0:T(8,128)}, u32[]{:S(2)}) copy-start(f32[64,512]{1,0:T(8,128)} %get-tuple-element.24) | copy-start | bytes 393220

commit v3 on v2

--- a/solution.py
+++ b/solution.py
@@ -66,6 +66,15 @@
     return high, (value - high.astype(F32)).astype(BF16)
 
 
+def multiple(value, of):
+    return value if isinstance(value, int) else pl.multiple_of(value, of)
+
+
+def unrolled(first, last, body):
+    for index in range(first, last):
+        body(index)
+
+
 def loop(first, last, body):
     def step(index, carry):
         body(index)
@@ -85,7 +94,7 @@
     pair_s, pair_r, taps_r,
     y, zh, zl, spec_t, spec_p, e, wh, wl,
     gf_s, gf_r, mm_s, mm_r,
-    part_s, rs_r, ga1, ga2, gav, sal_s, sal_r, o1, o2, ov, osal, osk,
+    part_s, rs_r, first_tile, sal_s, sal_r, o1, o2, ov, osal, osk,
     load_sem, out_sem, send_sem, recv_sem, halo_send, halo_recv, sal_send, sal_recv,
 ):
     me = lax.axis_index("seq")
@@ -112,12 +121,12 @@
         barrier, inc=1, device_id=(me, lax.rem(chan + i, 8)), device_id_type=MESH))
 
     def block_of(ref):
-        return lambda to: ref.at[pl.ds(pl.multiple_of(to * 32, 32), 32)]
+        return lambda to: ref.at[pl.ds(multiple(to * 32, 32), 32)]
 
     def slot_of(ref):
         return lambda to: ref.at[to]
 
-    def send_all(kind, source, target):
+    def send_all(kind, source, target, begin=1, end=16):
         def one(i):
             to = lax.rem(me + i, 16)
             pltpu.make_async_remote_copy(
@@ -126,8 +135,9 @@
                 device_id=(to, chan), device_id_type=MESH,
             ).start()
 
-        loop(1, 16, one)
-        pltpu.make_async_copy(source(me), target.at[me], recv_sem.at[kind]).start()
+        loop(begin, end, one)
+        if end == 16:
+            pltpu.make_async_copy(source(me), target.at[me], recv_sem.at[kind]).start()
 
     def wait_bytes(ref, sem):
         pltpu.make_async_copy(ref, ref, sem).wait()
@@ -137,7 +147,10 @@
             src_ref=source, dst_ref=target, send_sem=halo_send.at[n], recv_sem=halo_recv.at[n],
             device_id=(to, chan), device_id_type=MESH)
 
-    for n in range(6):
+    pl.semaphore_wait(barrier, 22)
+    send_all(0, block_of(taps_h), taps_r, 1, 7)
+
+    for n in range(3):
         loads[n].wait()
     row = lax.broadcasted_iota(jnp.int32, (16, 128), 0)
     lane = lax.broadcasted_iota(jnp.int32, (16, 128), 1)
@@ -146,11 +159,11 @@
         pick = ((row == 2 * s) & (lane == 126)) | ((row == 2 * s + 1) & (lane == 127))
         tails += dot_nt(pick.astype(F32).astype(BF16), ref[:, 384:512])
     tail_s[...] = tails.astype(BF16)
-
-    pl.semaphore_wait(barrier, 22)
     tail_copy = neighbour(tail_s, tail_r, 0, following)
     tail_copy.start()
-    send_all(0, block_of(taps_h), taps_r)
+    send_all(0, block_of(taps_h), taps_r, 7, 16)
+    for n in range(3, 6):
+        loads[n].wait()
 
     wrow[...] = jnp.zeros((128, 512), F32)
     for s in range(3):
@@ -165,7 +178,7 @@
     lane16 = lax.broadcasted_iota(jnp.int32, (16, 512), 1)
 
     def rows_of(block, h):
-        return pl.ds(pl.multiple_of(block * 32 + h * 16, 16), 16)
+        return pl.ds(multiple(block * 32 + h * 16, 16), 16)
 
     def gate(h):
         def body(block):
@@ -197,15 +210,15 @@
     for h in range(2):
         gate(h)
         send_all(1 + h, slot_of(pair_s.at[h]), pair_r.at[h])
-    swap = neighbour(sk_h, sk.at[core], 2, sibling)
+    swap = neighbour(sk_h, sk.at[core], 3, sibling)
     swap.start()
 
     def first_rows(tile, part, k1):
-        return y[tile, pl.ds(pl.multiple_of(part * 256 + k1 * 16, 16), 16), :]
+        return y[tile, pl.ds(multiple(part * 256 + k1 * 16, 16), 16), :]
 
     def store_z(index, re, im):
         for g in range(2):
-            rows = pl.ds(pl.multiple_of(index * 32 + g * 16, 16), 16)
+            rows = pl.ds(multiple(index * 32 + g * 16, 16), 16)
             side = slice(g * 128, g * 128 + 128)
             high, low = halves(jnp.concatenate([re[:, side], im[:, side]], axis=1))
             zh[rows, :] = high
@@ -217,11 +230,11 @@
 
     def forward(source, spec):
         def stage(tile):
-            lanes = pl.ds(pl.multiple_of(tile * 128, 128), 128)
+            lanes = pl.ds(multiple(tile * 128, 128), 128)
             right = jnp.concatenate([source(g, lanes).reshape(256, 128) for g in range(2)], axis=1)
             y[tile] = dot(c1h[tile], right) + dot(c1l[tile], right)
 
-        loop(0, 4, stage)
+        unrolled(0, 4, stage)
 
         def butterfly(k1):
             r0, r1, r2, r3 = [first_rows(t, 0, k1) for t in range(4)]
@@ -234,7 +247,7 @@
             twist(base + 2, ar - cr, ai - ci)
             twist(base + 3, br - di, bi + dr)
 
-        loop(1, 16, butterfly)
+        unrolled(1, 16, butterfly)
         r0, r1, r2, r3 = [first_rows(t, 0, 0) for t in range(4)]
         none = jnp.zeros_like(r0)
         store_z(60, r0 + r1 + r2 + r3, none)
@@ -245,11 +258,11 @@
         twist(64, r0 - ROOT * (r1 - r3), r2 - ROOT * (r1 + r3))
 
         def last(chunk):
-            rows = pl.ds(pl.multiple_of(chunk * 416, 16), 416)
+            rows = pl.ds(multiple(chunk * 416, 16), 416)
             out = dot(zh[rows, :], mh[...]) + dot(zl[rows, :], mh[...]) + dot(zh[rows, :], ml[...])
             spec[pl.ds(chunk * 13, 13)] = out.reshape(13, 32, 256)
 
-        loop(0, 5, last)
+        unrolled(0, 5, last)
 
     def times(left, right, sign):
         lr, li = left[..., 0:128], left[..., 128:256] * sign
@@ -262,20 +275,20 @@
 
         def first(chunk):
             high, low = halves(product(pl.ds(chunk * 13, 13)).reshape(13 * size, 256))
-            rows = pl.ds(pl.multiple_of(chunk * 13 * size, 16), 13 * size)
+            rows = pl.ds(multiple(chunk * 13 * size, 16), 13 * size)
             e[rows, :] = dot(high, nh[...]) + dot(low, nh[...]) + dot(high, nl[...])
 
-        loop(0, 5, first)
+        unrolled(0, 5, first)
 
         def untwist(index):
             cos, sin = twc[pl.ds(index, 1), :][:, 0:wide], tws[pl.ds(index, 1), :][:, 0:wide]
-            parts = [e[pl.ds(pl.multiple_of(index * size + 16 * g, 16), 16), :] for g in range(count)]
+            parts = [e[pl.ds(multiple(index * size + 16 * g, 16), 16), :] for g in range(count)]
             re = jnp.concatenate([p[:, 0:128] for p in parts], axis=1)
             im = jnp.concatenate([p[:, 128:256] for p in parts], axis=1)
             return re * cos - im * sin, im * cos + re * sin
 
         def store_w(tile, part, k1, value):
-            rows = pl.ds(pl.multiple_of(part * 256 + k1 * 16, 16), 16)
+            rows = pl.ds(multiple(part * 256 + k1 * 16, 16), 16)
             high, low = halves(value)
             wh[tile, rows, 0:wide] = high
             wl[tile, rows, 0:wide] = low
@@ -294,7 +307,7 @@
             store_w(3, 0, k1, br + di)
             store_w(3, 1, k1, bi - dr)
 
-        loop(1, 16, butterfly)
+        unrolled(1, 16, butterfly)
         (r0, _), (r32, i32), (r64, _), (r16, i16), (r48, i48) = [untwist(60 + n) for n in range(5)]
         plus, minus = 0.5 * (r0 + r64), 0.5 * (r0 - r64)
         store_w(0, 0, 0, plus + r32)
@@ -307,42 +320,41 @@
         store_w(3, 1, 0, ROOT * (r48 - i48 - r16 - i16))
 
         def last(tile):
-            lanes = pl.ds(pl.multiple_of(tile * 128, 128), 128)
+            lanes = pl.ds(multiple(tile * 128, 128), 128)
             high, low = wh[tile, :, 0:wide], wl[tile, :, 0:wide]
             out = (dot(dh[tile], high) + dot(dh[tile], low) + dot(dl[tile], high)).astype(BF16)
             for g in range(count):
                 store(g, lanes, out[:, g * 128 : g * 128 + 128].reshape(16, 16, 128))
 
-        loop(0, 4, last)
-
-    def filter_copy(h, chip):
-        return pltpu.make_async_remote_copy(
-            src_ref=gf_s.at[h, pl.ds(2 * chip, 2)], dst_ref=gf_r.at[me - 8 * half, h],
-            send_sem=send_sem.at[3 + h], recv_sem=recv_sem.at[3 + h],
-            device_id=(2 * chip + half, chan), device_id_type=MESH)
-
-    def filter_out(h):
+        unrolled(0, 4, last)
+
+    def filter_out():
         def product(index):
-            return times(spec_p[h, index, 16:32, :], spec_p[h, index, 0:16, :], -1.0)
+            return jnp.concatenate(
+                [times(spec_p[h, index, 16:32, :], spec_p[h, index, 0:16, :], -1.0) for h in range(2)],
+                axis=1)
 
         def store(g, lanes, value):
-            gf_s[h, :, :, lanes] = value
-
-        inverse(product, 1, store)
+            gf_s[:, g * 16 : g * 16 + 16, lanes] = value
+
+        inverse(product, 2, store)
 
         def one(n):
             chip = lax.rem(me // 2 + n, 8)
 
             @pl.when(2 * chip + half != me)
             def _():
-                filter_copy(h, chip).start()
+                pltpu.make_async_remote_copy(
+                    src_ref=gf_s.at[pl.ds(2 * chip, 2)], dst_ref=gf_r.at[me - 8 * half],
+                    send_sem=send_sem.at[3], recv_sem=recv_sem.at[3],
+                    device_id=(2 * chip + half, chan), device_id_type=MESH).start()
 
         loop(0, 8, one)
 
         @pl.when(core == half)
         def _():
             pltpu.make_async_copy(
-                gf_s.at[h, pl.ds(2 * (me // 2), 2)], gf_r.at[me - 8 * half, h], recv_sem.at[3 + h]).start()
+                gf_s.at[pl.ds(2 * (me // 2), 2)], gf_r.at[me - 8 * half], recv_sem.at[3]).start()
 
     def mixes_out(h):
         def product(index):
@@ -355,7 +367,7 @@
             mm_s[h, :, g, :, lanes] = value
 
         inverse(product, 2, store)
-        send_all(5 + h, slot_of(mm_s.at[h]), mm_r.at[h])
+        send_all(4 + h, slot_of(mm_s.at[h]), mm_r.at[h])
 
     for n in range(6, 16):
         loads[n].wait()
@@ -364,73 +376,86 @@
     for h in range(2):
         wait_bytes(pair_r.at[h], recv_sem.at[1 + h])
         forward(lambda g, lanes: pair_r[h, :, g, :, lanes], spec_p.at[h])
-        filter_out(h)
+        if h == 1:
+            filter_out()
         mixes_out(h)
 
-    def activations(h):
-        wait_bytes(mm_r.at[h], recv_sem.at[5 + h])
+    def activations(h, block, lanes):
+        rows = rows_of(block, h)
+        skip = wcol[rows, 9:10]
+        mixed = mm_r[h, block, 0, :, lanes].astype(F32) + skip * pair_s[h, block, 1, :, lanes].astype(F32)
+        grad_mix = mm_r[h, block, 1, :, lanes].astype(F32) + skip * pair_s[h, block, 0, :, lanes].astype(F32)
+        return (
+            go[rows, lanes].astype(F32) * mixed,
+            grad_mix * actv[rows, lanes],
+            grad_mix * act2[rows, lanes],
+        )
+
+    def edge_copy(h):
+        return neighbour(edge_s.at[h], edge_r.at[h], 1 + h, previous)
+
+    def edges_out(h):
+        wait_bytes(mm_r.at[h], recv_sem.at[4 + h])
+
+        def body(block):
+            for s, value in enumerate(activations(h, block, slice(0, 128))):
+                first_tile[s, pl.ds(multiple(block * 16, 16), 16), :] = value.astype(BF16)
+
+        loop(0, 16, body)
+        edges = jnp.zeros((16, 256), F32)
+        for s in range(3):
+            pick = ((row == 2 * s) & (lane == 0)) | ((row == 2 * s + 1) & (lane == 1))
+            edges += dot_nt(pick.astype(F32).astype(BF16), first_tile[s])
+        edge_s[h] = edges.astype(BF16)
+        edge_copy(h).start()
+
+    def adjoint(h):
+        edge_copy(h).wait_recv()
+        wrow[0:16, 0:256] = edge_r[h].astype(F32) * (me < 15).astype(F32)
+        hcol[0:256, :] = jnp.transpose(wrow[:, 0:256])
 
         def body(block):
             rows = rows_of(block, h)
-            skip = wcol[rows, 9:10]
-            mixed = mm_r[h, block, 0].astype(F32) + skip * pair_s[h, block, 1].astype(F32)
-            ga1[rows, :] = go[rows, :].astype(F32) * mixed
-            grad_mix = mm_r[h, block, 1].astype(F32) + skip * pair_s[h, block, 0].astype(F32)
-            ga2[rows, :] = grad_mix * actv[rows, :]
-            gav[rows, :] = grad_mix * act2[rows, :]
+            weight = wcol[rows, :]
+            halo = hcol[pl.ds(multiple(block * 16, 16), 16), :]
+            total = jnp.zeros((16, 512), F32)
+            fields = activations(h, block, slice(0, 512))
+            for s, (field, stream, out) in enumerate(zip(fields, (x1, x2, xv), (o1, o2, ov))):
+                next_one, next_two = halo[:, 2 * s : 2 * s + 1], halo[:, 2 * s + 1 : 2 * s + 2]
+                one = jnp.where(lane16 == 511, next_one, pltpu.roll(field, 511, 1))
+                two = jnp.where(
+                    lane16 == 511, next_two, jnp.where(lane16 == 510, next_one, pltpu.roll(field, 510, 1)))
+                full = (
+                    weight[:, 3 * s : 3 * s + 1] * field
+                    + weight[:, 3 * s + 1 : 3 * s + 2] * one
+                    + weight[:, 3 * s + 2 : 3 * s + 3] * two
+                )
+                out[rows, :] = full.astype(BF16)
+                total += stream[rows, :].astype(F32) * full
+            sal_s[...] += total[0:8] + total[8:16]
 
         loop(0, 16, body)
 
+    edges_out(0)
+
     loads[16].wait()
-    swap_in = neighbour(sk_h, sk.at[1 - core], 2, sibling)
+    swap_in = neighbour(sk_h, sk.at[1 - core], 3, sibling)
     swap_in.wait_recv()
-    for h in range(2):
-        wait_bytes(gf_s.at[h], recv_sem.at[3 + h])
+    wait_bytes(gf_s, recv_sem.at[3])
 
     def sketch_rows(block):
-        rows = pl.ds(pl.multiple_of(block * 256, 256), 256)
-        total = dot_nt(sk[0, rows, :], gf_r[:, :, 0].reshape(256, 512))
-        total += dot_nt(sk[1, rows, :], gf_r[:, :, 1].reshape(256, 512))
+        rows = pl.ds(block * 256, 256)
+        total = dot_nt(sk[0, rows, :], gf_r[:, 0].reshape(256, 512))
+        total += dot_nt(sk[1, rows, :], gf_r[:, 1].reshape(256, 512))
         part_s[pl.ds(block * 4, 4)] = total.astype(BF16).reshape(4, 64, 256)
 
-    loop(0, 4, sketch_rows)
-    send_all(7, slot_of(part_s), rs_r)
-
-    activations(0)
-    activations(1)
-    edges = jnp.zeros((16, 512), F32)
-    for s, ref in enumerate((ga1, ga2, gav)):
-        pick = ((row == 2 * s) & (lane == 0)) | ((row == 2 * s + 1) & (lane == 1))
-        edges += dot_nt(pick.astype(F32).astype(BF16), ref[:, 0:128].astype(BF16))
-    edge_s[...] = edges.astype(BF16)
-    edge_copy = neighbour(edge_s, edge_r, 1, previous)
-    edge_copy.start()
-    edge_copy.wait_recv()
-    wrow[0:16, :] = edge_r[...].astype(F32) * (me < 15).astype(F32)
-    hcol[...] = jnp.transpose(wrow[...])
+    unrolled(0, 4, sketch_rows)
+    send_all(6, slot_of(part_s), rs_r, 1, 8)
     sal_s[...] = jnp.zeros((8, 512), F32)
-
-    def adjoint(block):
-        rows = pl.ds(pl.multiple_of(block * 16, 16), 16)
-        weight = wcol[rows, :]
-        halo = hcol[rows, :]
-        total = jnp.zeros((16, 512), F32)
-        for s, (grad, stream, out) in enumerate(((ga1, x1, o1), (ga2, x2, o2), (gav, xv, ov))):
-            field = grad[rows, :]
-            next_one, next_two = halo[:, 2 * s : 2 * s + 1], halo[:, 2 * s + 1 : 2 * s + 2]
-            one = jnp.where(lane16 == 511, next_one, pltpu.roll(field, 511, 1))
-            two = jnp.where(
-                lane16 == 511, next_two, jnp.where(lane16 == 510, next_one, pltpu.roll(field, 510, 1)))
-            full = (
-                weight[:, 3 * s : 3 * s + 1] * field
-                + weight[:, 3 * s + 1 : 3 * s + 2] * one
-                + weight[:, 3 * s + 2 : 3 * s + 3] * two
-            )
-            out[rows, :] = full.astype(BF16)
-            total += stream[rows, :].astype(F32) * full
-        sal_s[...] += total[0:8] + total[8:16]
-
-    loop(0, 32, adjoint)
+    adjoint(0)
+    edges_out(1)
+    send_all(6, slot_of(part_s), rs_r, 8, 16)
+    adjoint(1)
     outs = [
         pltpu.make_async_copy(a, b, out_sem.at[n])
         for n, (a, b) in enumerate(((o1, o1_h), (o2, o2_h), (ov, ov_h), (osk, osk_h), (osal, osal_h)))
@@ -446,7 +471,7 @@
     loop(1, 8, sal_send_to)
     pltpu.make_async_copy(sal_s, sal_r.at[chan], sal_recv.at[0]).start()
 
-    wait_bytes(rs_r, recv_sem.at[7])
+    wait_bytes(rs_r, recv_sem.at[6])
     for side in range(2):
         total = rs_r[side].astype(F32)
         for chip in range(1, 8):
@@ -464,22 +489,36 @@
     outs[4].start()
 
     tail_copy.wait_send()
-    edge_copy.wait_send()
     swap.wait_send()
     wait_bytes(taps_r.at[pl.ds(0, 15)], send_sem.at[0])
     for h in range(2):
+        edge_copy(h).wait_send()
         wait_bytes(pair_s.at[h, pl.ds(0, 15)], send_sem.at[1 + h])
-        wait_bytes(mm_s.at[h, pl.ds(0, 15)], send_sem.at[5 + h])
-        wait_bytes(gf_s.at[h, pl.ds(0, 14)], send_sem.at[3 + h])
-
-        @pl.when(core != half)
-        def _():
-            wait_bytes(gf_s.at[h, pl.ds(14, 2)], send_sem.at[3 + h])
-
-    wait_bytes(part_s.at[pl.ds(0, 15)], send_sem.at[7])
+        wait_bytes(mm_s.at[h, pl.ds(0, 15)], send_sem.at[4 + h])
+    wait_bytes(gf_s.at[pl.ds(0, 14)], send_sem.at[3])
+
+    @pl.when(core != half)
+    def _():
+        wait_bytes(gf_s.at[pl.ds(14, 2)], send_sem.at[3])
+
+    wait_bytes(part_s.at[pl.ds(0, 15)], send_sem.at[6])
     wait_bytes(sal_r.at[pl.ds(0, 7)], sal_send.at[0])
     for out in outs:
         out.wait()
+
+
+def finish(a1, a2, av, asal, ask, b1, b2, bv, bsal, bsk, c1, c2, cv, ck, in_sem, out_sem):
+    stages = ((a1, c1, b1), (a2, c2, b2), (av, cv, bv), (ask, ck, bsk))
+    ins = [pltpu.make_async_copy(a, c, in_sem.at[n]) for n, (a, c, _) in enumerate(stages)]
+    outs = [pltpu.make_async_copy(c, b, out_sem.at[n]) for n, (_, c, b) in enumerate(stages)]
+    for copy in ins:
+        copy.start()
+    bsal[...] = asal[0, 0:64]
+    for first, second in zip(ins, outs):
+        first.wait()
+        second.start()
+    for copy in outs:
+        copy.wait()
 
 
 def on_device(*arrays):
@@ -496,22 +535,22 @@
         *[vmem(square) for _ in range(4)], vmem((3, 3, 512), F32), vmem((1, 512), F32), vmem((2, 1024, 512)),
         *[vmem(t.shape, t.dtype) for t in tables],
         vmem((128, 512), F32), vmem((512, 128), F32),
-        vmem((16, 512)), vmem((16, 512)), vmem((16, 512)), vmem((16, 512)), vmem((512, 128), F32),
+        vmem((16, 512)), vmem((16, 512)), vmem((2, 16, 256)), vmem((2, 16, 256)), vmem((512, 128), F32),
         vmem(square, F32), vmem(square, F32),
         vmem(parts), vmem(parts), vmem((16, 32, 512)),
         vmem((4, 512, 256), F32), vmem((ROWS, 256)), vmem((ROWS, 256)),
         vmem((65, 32, 256), F32), vmem((2, 65, 32, 256), F32), vmem((ROWS, 256), F32),
         vmem((4, 512, 256)), vmem((4, 512, 256)),
-        vmem((2, 16, 16, 512)), vmem((8, 2, 2, 16, 512)), vmem(parts), vmem(parts),
+        vmem((16, 32, 512)), vmem((8, 2, 32, 512)), vmem(parts), vmem(parts),
         vmem((16, 64, 256)), vmem((16, 64, 256)),
-        *[vmem(square, F32) for _ in range(3)], vmem((8, 512), F32), vmem((8, 8, 512), F32),
+        vmem((3, 256, 128)), vmem((8, 512), F32), vmem((8, 8, 512), F32),
         *[vmem(square) for _ in range(3)], vmem((8, 128), F32), vmem((64, 512), F32),
         pltpu.SemaphoreType.DMA((17,)), pltpu.SemaphoreType.DMA((5,)),
-        pltpu.SemaphoreType.DMA((8,)), pltpu.SemaphoreType.DMA((8,)),
-        pltpu.SemaphoreType.DMA((3,)), pltpu.SemaphoreType.DMA((3,)),
+        pltpu.SemaphoreType.DMA((7,)), pltpu.SemaphoreType.DMA((7,)),
+        pltpu.SemaphoreType.DMA((4,)), pltpu.SemaphoreType.DMA((4,)),
         pltpu.SemaphoreType.DMA((1,)), pltpu.SemaphoreType.DMA((1,)),
     ]
-    grad_one, grad_two, grad_value, saliency, sketched = pl.pallas_call(
+    results = pl.pallas_call(
         kernel,
         out_shape=[
             *[jax.ShapeDtypeStruct(square, BF16) for _ in range(3)],
@@ -524,7 +563,22 @@
         compiler_params=pltpu.CompilerParams(
             collective_id=0, has_side_effects=True, vmem_limit_bytes=56 * 1024 * 1024),
     )(*operands)
-    return grad_one, grad_two, grad_value, saliency[0, :64], sketched
+    anywhere = pl.BlockSpec(memory_space=pl.ANY)
+    near = pl.BlockSpec(memory_space=pltpu.VMEM)
+    return pl.pallas_call(
+        finish,
+        out_shape=[
+            *[jax.ShapeDtypeStruct(square, BF16) for _ in range(3)],
+            jax.ShapeDtypeStruct((64,), F32),
+            jax.ShapeDtypeStruct((64, 512), F32),
+        ],
+        in_specs=[anywhere, anywhere, anywhere, near, anywhere],
+        out_specs=[anywhere, anywhere, anywhere, near, anywhere],
+        scratch_shapes=[
+            *[vmem(square) for _ in range(3)], vmem((64, 512), F32),
+            pltpu.SemaphoreType.DMA((4,)), pltpu.SemaphoreType.DMA((4,)),
+        ],
+    )(*results)
 
 
 def solution(mesh):

time: 77.8 us -> 70 us (0.90)
  local copies, waits for them, and re-layouts: 6.03 us -> 0 us
  Pallas kernels: 70.9 us -> 69.1 us
    pallas_call x1, Pallas kernels: 70.9 us -> 65.6 us  [on_device(): pl.pallas_call(kernel, out_shape=[*[jax.ShapeDtypeStruct(square, BF16) fo...]
    unnamed x10 -> x0, local copies, waits for them, and re-layouts: 4.84 us -> none
    pallas_call x0 -> x1, Pallas kernels: none -> 3.47 us  [on_device(): pl.pallas_call(finish, out_shape=[*[jax.ShapeDtypeStruct(square, BF16) fo...]
    squeeze x1 -> x0, local copies, waits for them, and re-layouts: 1.19 us -> none  [on_device(): return (grad_one, grad_two, grad_value, saliency[0, :64], sketched)]
where the time goes in v3:
time: 70 us; the launch traced here: 69.9 us
  Pallas kernels  69.1 us (99%)
  between operations  0.8 us (1%)
    pallas_call x1, Pallas kernels, on_device(): pl.pallas_call(kernel, out_shape=[*[jax.ShapeDtypeStruct(square, BF16) fo...  65.6 us
    pallas_call x1, Pallas kernels, on_device(): pl.pallas_call(finish, out_shape=[*[jax.ShapeDtypeStruct(square, BF16) fo...  3.47 us

profile of v3, /device:TPU:1, one launch (start us, length us, event | category | flops | bytes accessed | tf_op | source)
XLA Modules:
  0.0 69.9 jit_solution(11886165663992629249)
XLA Ops:
  0.6 65.6 %shard_map.209 = (bf16[512,512]{1,0:T(8,128)(2,1)}, bf16[512,512]{1,0:T(8,128)(2,1)}, bf16[512,512]{1,0:T(8,128)(2,1)}, f32[8,128]{1,0:T(8,128)}, f32[64,512]{1,0:T(8,128)}) custom-call(bf16[512,512]{1,0:T(8,128)(2,1)} %x1_h.1, bf16[512,512]{1,0:T(8,128)(2,1)} %x2_h.1, bf16[512,512]{1,0:T(8,128)(2,1)} %xv_h.1, bf16[512,512]{1,0:T(8,128)(2,1)} %go_h.1, ...), custom_call_target="tpu_custom_call" | custom-call | tf_op jit(solution)/shard_map/pallas_call | solution.py:553
  66.2 3.5 %shard_map.210 = (bf16[512,512]{1,0:T(8,128)(2,1)}, bf16[512,512]{1,0:T(8,128)(2,1)}, bf16[512,512]{1,0:T(8,128)(2,1)}, f32[64]{0:T(128)}, f32[64,512]{1,0:T(8,128)}) custom-call(bf16[512,512]{1,0:T(8,128)(2,1)} %get-tuple-element.10.a1, bf16[512,512]{1,0:T(8,128)(2,1)} %get-tuple-element.11.a2, bf16[512,512]{1,0:T(8,128)(2,1)} %get-tuple-element.12.av, ...), custom_call_target="tpu_custom_call" | custom-call | tf_op jit(solution)/shard_map/pallas_call | solution.py:568

commit v4 on v3

--- a/solution.py
+++ b/solution.py
@@ -89,12 +89,12 @@
     o1_h, o2_h, ov_h, osal_h, osk_h,
     x1, x2, xv, go, short, gain, sk,
     c1h, c1l, dh, dl, mh, ml, nh, nl, twc, tws,
-    wrow, wcol, tail_s, tail_r, edge_s, edge_r, hcol,
+    wrow, wcol, tail_s, tail_r, head_s, head_r, hcol, head_tile, head_gate, head_mult,
     act2, actv,
     pair_s, pair_r, taps_r,
     y, zh, zl, spec_t, spec_p, e, wh, wl,
     gf_s, gf_r, mm_s, mm_r,
-    part_s, rs_r, first_tile, sal_s, sal_r, o1, o2, ov, osal, osk,
+    part_s, rs_r, sal_s, sal_r, o1, o2, ov, osal, osk,
     load_sem, out_sem, send_sem, recv_sem, halo_send, halo_recv, sal_send, sal_recv,
 ):
     me = lax.axis_index("seq")
@@ -198,20 +198,36 @@
                 )
 
             first = short_filter(x1, 0)
-            pair_s[h, block, 0] = (go[rows, :].astype(F32) * first).astype(BF16)
+            grad = go[rows, :]
+            pair_s[h, block, 0] = (grad.astype(F32) * first).astype(BF16)
             second = short_filter(x2, 1)
             value = short_filter(xv, 2)
             act2[rows, :] = second
             actv[rows, :] = value
             pair_s[h, block, 1] = (second * value).astype(BF16)
+            spot = pl.ds(multiple(block * 16, 16), 16)
+            head_tile[h, 0, spot, :] = pair_s[h, block, 1, :, 0:128]
+            head_tile[h, 1, spot, :] = pair_s[h, block, 0, :, 0:128]
+            head_tile[h, 2, spot, :] = grad[:, 0:128]
+            head_tile[h, 3, spot, :] = value[:, 0:128].astype(BF16)
+            head_tile[h, 4, spot, :] = second[:, 0:128].astype(BF16)
 
         loop(0, 16, body)
 
     for h in range(2):
         gate(h)
         send_all(1 + h, slot_of(pair_s.at[h]), pair_r.at[h])
-    swap = neighbour(sk_h, sk.at[core], 3, sibling)
+    swap = neighbour(sk_h, sk.at[core], 2, sibling)
     swap.start()
+
+    for h in range(2):
+        heads = jnp.zeros((16, 256), F32)
+        for at, n in ((0, 0), (2, 1), (4, 1), (6, 2), (8, 3), (10, 4)):
+            pick = ((row == at) & (lane == 0)) | ((row == at + 1) & (lane == 1))
+            heads += dot_nt(pick.astype(F32).astype(BF16), head_tile[h, n])
+        head_s[h] = heads.astype(BF16)
+    head_copy = neighbour(head_s, head_r, 1, previous)
+    head_copy.start()
 
     def first_rows(tile, part, k1):
         return y[tile, pl.ds(multiple(part * 256 + k1 * 16, 16), 16), :]
@@ -269,7 +285,7 @@
         rr, ri = right[..., 0:128], right[..., 128:256]
         return jnp.concatenate([lr * rr - li * ri, lr * ri + li * rr], axis=2)
 
-    def inverse(product, count, store):
+    def inverse(product, count, store, more=None):
         size = 16 * count
         wide = 128 * count
 
@@ -320,11 +336,12 @@
         store_w(3, 1, 0, ROOT * (r48 - i48 - r16 - i16))
 
         def last(tile):
-            lanes = pl.ds(multiple(tile * 128, 128), 128)
             high, low = wh[tile, :, 0:wide], wl[tile, :, 0:wide]
-            out = (dot(dh[tile], high) + dot(dh[tile], low) + dot(dl[tile], high)).astype(BF16)
+            out = dot(dh[tile], high) + dot(dh[tile], low) + dot(dl[tile], high)
             for g in range(count):
-                store(g, lanes, out[:, g * 128 : g * 128 + 128].reshape(16, 16, 128))
+                store(g, tile, out[:, g * 128 : g * 128 + 128].astype(BF16).reshape(16, 16, 128))
+            if more is not None and tile == 0:
+                more(out)
 
         unrolled(0, 4, last)
 
@@ -334,8 +351,8 @@
                 [times(spec_p[h, index, 16:32, :], spec_p[h, index, 0:16, :], -1.0) for h in range(2)],
                 axis=1)
 
-        def store(g, lanes, value):
-            gf_s[:, g * 16 : g * 16 + 16, lanes] = value
+        def store(g, tile, value):
+            gf_s[:, g * 16 : g * 16 + 16, tile * 128 : tile * 128 + 128] = value
 
         inverse(product, 2, store)
 
@@ -363,10 +380,17 @@
                 [times(taps, spec_p[h, index, 16:32, :], 1.0), times(taps, spec_p[h, index, 0:16, :], -1.0)],
                 axis=1)
 
-        def store(g, lanes, value):
-            mm_s[h, :, g, :, lanes] = value
-
-        inverse(product, 2, store)
+        def store(g, tile, value):
+            mm_s[h, :, 4 * g + tile] = value
+
+        def more(out):
+            mixed, grad_mix = out[16:256, 0:128], out[16:256, 128:256]
+            side = lax.broadcasted_iota(jnp.int32, (240, 128), 1)
+            value = jnp.where(side < 2, mixed, jnp.where(side < 4, pltpu.roll(grad_mix, 2, 1), pltpu.roll(grad_mix, 4, 1)))
+            mm_s[h, 0:15, 8] = value.astype(BF16).reshape(15, 16, 128)
+            mm_s[h, 15, 8] = jnp.zeros((16, 128), BF16)
+
+        inverse(product, 2, store, more)
         send_all(4 + h, slot_of(mm_s.at[h]), mm_r.at[h])
 
     for n in range(6, 16):
@@ -380,46 +404,22 @@
             filter_out()
         mixes_out(h)
 
-    def activations(h, block, lanes):
-        rows = rows_of(block, h)
-        skip = wcol[rows, 9:10]
-        mixed = mm_r[h, block, 0, :, lanes].astype(F32) + skip * pair_s[h, block, 1, :, lanes].astype(F32)
-        grad_mix = mm_r[h, block, 1, :, lanes].astype(F32) + skip * pair_s[h, block, 0, :, lanes].astype(F32)
-        return (
-            go[rows, lanes].astype(F32) * mixed,
-            grad_mix * actv[rows, lanes],
-            grad_mix * act2[rows, lanes],
-        )
-
-    def edge_copy(h):
-        return neighbour(edge_s.at[h], edge_r.at[h], 1 + h, previous)
-
-    def edges_out(h):
+    def adjoint(h):
         wait_bytes(mm_r.at[h], recv_sem.at[4 + h])
-
-        def body(block):
-            for s, value in enumerate(activations(h, block, slice(0, 128))):
-                first_tile[s, pl.ds(multiple(block * 16, 16), 16), :] = value.astype(BF16)
-
-        loop(0, 16, body)
-        edges = jnp.zeros((16, 256), F32)
-        for s in range(3):
-            pick = ((row == 2 * s) & (lane == 0)) | ((row == 2 * s + 1) & (lane == 1))
-            edges += dot_nt(pick.astype(F32).astype(BF16), first_tile[s])
-        edge_s[h] = edges.astype(BF16)
-        edge_copy(h).start()
-
-    def adjoint(h):
-        edge_copy(h).wait_recv()
-        wrow[0:16, 0:256] = edge_r[h].astype(F32) * (me < 15).astype(F32)
-        hcol[0:256, :] = jnp.transpose(wrow[:, 0:256])
 
         def body(block):
             rows = rows_of(block, h)
             weight = wcol[rows, :]
-            halo = hcol[pl.ds(multiple(block * 16, 16), 16), :]
+            skip = weight[:, 9:10]
+            spot = pl.ds(multiple(block * 16, 16), 16)
+            halo = head_mult[h, spot, :] * (mm_r[h, block, 8].astype(F32) + skip * head_gate[h, spot, :])
+            mixed, grad_mix = [
+                jnp.concatenate([mm_r[h, block, 4 * g + tile] for tile in range(4)], axis=1).astype(F32)
+                + skip * pair_s[h, block, 1 - g].astype(F32)
+                for g in range(2)
+            ]
+            fields = (go[rows, :].astype(F32) * mixed, grad_mix * actv[rows, :], grad_mix * act2[rows, :])
             total = jnp.zeros((16, 512), F32)
-            fields = activations(h, block, slice(0, 512))
             for s, (field, stream, out) in enumerate(zip(fields, (x1, x2, xv), (o1, o2, ov))):
                 next_one, next_two = halo[:, 2 * s : 2 * s + 1], halo[:, 2 * s + 1 : 2 * s + 2]
                 one = jnp.where(lane16 == 511, next_one, pltpu.roll(field, 511, 1))
@@ -436,10 +436,8 @@
 
         loop(0, 16, body)
 
-    edges_out(0)
-
     loads[16].wait()
-    swap_in = neighbour(sk_h, sk.at[1 - core], 3, sibling)
+    swap_in = neighbour(sk_h, sk.at[1 - core], 2, sibling)
     swap_in.wait_recv()
     wait_bytes(gf_s, recv_sem.at[3])
 
@@ -450,11 +448,16 @@
         part_s[pl.ds(block * 4, 4)] = total.astype(BF16).reshape(4, 64, 256)
 
     unrolled(0, 4, sketch_rows)
-    send_all(6, slot_of(part_s), rs_r, 1, 8)
+    send_all(6, slot_of(part_s), rs_r)
     sal_s[...] = jnp.zeros((8, 512), F32)
+    head_copy.wait_recv()
+    for h in range(2):
+        heads = head_r[h].astype(F32) * (me < 15).astype(F32)
+        wrow[0:16, 0:256] = heads
+        head_gate[h] = jnp.transpose(wrow[:, 0:256])
+        wrow[0:16, 0:256] = pltpu.roll(heads, 10, 0)
+        head_mult[h] = jnp.transpose(wrow[:, 0:256])
     adjoint(0)
-    edges_out(1)
-    send_all(6, slot_of(part_s), rs_r, 8, 16)
     adjoint(1)
     outs = [
         pltpu.make_async_copy(a, b, out_sem.at[n])
@@ -490,9 +493,9 @@
 
     tail_copy.wait_send()
     swap.wait_send()
+    head_copy.wait_send()
     wait_bytes(taps_r.at[pl.ds(0, 15)], send_sem.at[0])
     for h in range(2):
-        edge_copy(h).wait_send()
         wait_bytes(pair_s.at[h, pl.ds(0, 15)], send_sem.at[1 + h])
         wait_bytes(mm_s.at[h, pl.ds(0, 15)], send_sem.at[4 + h])
     wait_bytes(gf_s.at[pl.ds(0, 14)], send_sem.at[3])
@@ -531,23 +534,25 @@
 
     square = (512, 512)
     parts = (2, 16, 2, 16, 512)
+    mixes = (2, 16, 9, 16, 128)
     scratch = [
         *[vmem(square) for _ in range(4)], vmem((3, 3, 512), F32), vmem((1, 512), F32), vmem((2, 1024, 512)),
         *[vmem(t.shape, t.dtype) for t in tables],
         vmem((128, 512), F32), vmem((512, 128), F32),
         vmem((16, 512)), vmem((16, 512)), vmem((2, 16, 256)), vmem((2, 16, 256)), vmem((512, 128), F32),
+        vmem((2, 5, 256, 128)), vmem((2, 256, 128), F32), vmem((2, 256, 128), F32),
         vmem(square, F32), vmem(square, F32),
         vmem(parts), vmem(parts), vmem((16, 32, 512)),
         vmem((4, 512, 256), F32), vmem((ROWS, 256)), vmem((ROWS, 256)),
         vmem((65, 32, 256), F32), vmem((2, 65, 32, 256), F32), vmem((ROWS, 256), F32),
         vmem((4, 512, 256)), vmem((4, 512, 256)),
-        vmem((16, 32, 512)), vmem((8, 2, 32, 512)), vmem(parts), vmem(parts),
+        vmem((16, 32, 512)), vmem((8, 2, 32, 512)), vmem(mixes), vmem(mixes),
         vmem((16, 64, 256)), vmem((16, 64, 256)),
-        vmem((3, 256, 128)), vmem((8, 512), F32), vmem((8, 8, 512), F32),
+        vmem((8, 512), F32), vmem((8, 8, 512), F32),
         *[vmem(square) for _ in range(3)], vmem((8, 128), F32), vmem((64, 512), F32),
         pltpu.SemaphoreType.DMA((17,)), pltpu.SemaphoreType.DMA((5,)),
         pltpu.SemaphoreType.DMA((7,)), pltpu.SemaphoreType.DMA((7,)),
-        pltpu.SemaphoreType.DMA((4,)), pltpu.SemaphoreType.DMA((4,)),
+        pltpu.SemaphoreType.DMA((3,)), pltpu.SemaphoreType.DMA((3,)),
         pltpu.SemaphoreType.DMA((1,)), pltpu.SemaphoreType.DMA((1,)),
     ]
     results = pl.pallas_call(

time: 70 us -> 65.5 us (0.936)
  Pallas kernels: 69.1 us -> 64.5 us
    pallas_call x1, Pallas kernels: 65.6 us -> 61.1 us  [on_device(): pl.pallas_call(kernel, out_shape=[*[jax.ShapeDtypeStruct(square, BF16) fo...]
where the time goes in v4:
time: 65.5 us; the launch traced here: 65.3 us
  Pallas kernels  64.5 us (98%)
  between operations  0.8 us (1%)
    pallas_call x1, Pallas kernels, on_device(): pl.pallas_call(kernel, out_shape=[*[jax.ShapeDtypeStruct(square, BF16) fo...  61.1 us
    pallas_call x1, Pallas kernels, on_device(): pl.pallas_call(finish, out_shape=[*[jax.ShapeDtypeStruct(square, BF16) fo...  3.47 us

profile of v4, /device:TPU:1, one launch (start us, length us, event | category | flops | bytes accessed | tf_op | source)
XLA Modules:
  0.0 65.3 jit_solution(608978631194166931)
XLA Ops:
  0.6 61.1 %shard_map.209 = (bf16[512,512]{1,0:T(8,128)(2,1)}, bf16[512,512]{1,0:T(8,128)(2,1)}, bf16[512,512]{1,0:T(8,128)(2,1)}, f32[8,128]{1,0:T(8,128)}, f32[64,512]{1,0:T(8,128)}) custom-call(bf16[512,512]{1,0:T(8,128)(2,1)} %x1_h.1, bf16[512,512]{1,0:T(8,128)(2,1)} %x2_h.1, bf16[512,512]{1,0:T(8,128)(2,1)} %xv_h.1, bf16[512,512]{1,0:T(8,128)(2,1)} %go_h.1, ...), custom_call_target="tpu_custom_call" | custom-call | tf_op jit(solution)/shard_map/pallas_call | solution.py:558
  61.7 3.5 %shard_map.210 = (bf16[512,512]{1,0:T(8,128)(2,1)}, bf16[512,512]{1,0:T(8,128)(2,1)}, bf16[512,512]{1,0:T(8,128)(2,1)}, f32[64]{0:T(128)}, f32[64,512]{1,0:T(8,128)}) custom-call(bf16[512,512]{1,0:T(8,128)(2,1)} %get-tuple-element.10.a1, bf16[512,512]{1,0:T(8,128)(2,1)} %get-tuple-element.11.a2, bf16[512,512]{1,0:T(8,128)(2,1)} %get-tuple-element.12.av, ...), custom_call_target="tpu_custom_call" | custom-call | tf_op jit(solution)/shard_map/pallas_call | solution.py:573

commit v5 on v4

--- a/solution.py
+++ b/solution.py
@@ -126,7 +126,7 @@
     def slot_of(ref):
         return lambda to: ref.at[to]
 
-    def send_all(kind, source, target, begin=1, end=16):
+    def send_all(kind, source, target):
         def one(i):
             to = lax.rem(me + i, 16)
             pltpu.make_async_remote_copy(
@@ -135,9 +135,8 @@
                 device_id=(to, chan), device_id_type=MESH,
             ).start()
 
-        loop(begin, end, one)
-        if end == 16:
-            pltpu.make_async_copy(source(me), target.at[me], recv_sem.at[kind]).start()
+        loop(1, 16, one)
+        pltpu.make_async_copy(source(me), target.at[me], recv_sem.at[kind]).start()
 
     def wait_bytes(ref, sem):
         pltpu.make_async_copy(ref, ref, sem).wait()
@@ -146,9 +145,6 @@
         return pltpu.make_async_remote_copy(
             src_ref=source, dst_ref=target, send_sem=halo_send.at[n], recv_sem=halo_recv.at[n],
             device_id=(to, chan), device_id_type=MESH)
-
-    pl.semaphore_wait(barrier, 22)
-    send_all(0, block_of(taps_h), taps_r, 1, 7)
 
     for n in range(3):
         loads[n].wait()
@@ -159,9 +155,11 @@
         pick = ((row == 2 * s) & (lane == 126)) | ((row == 2 * s + 1) & (lane == 127))
         tails += dot_nt(pick.astype(F32).astype(BF16), ref[:, 384:512])
     tail_s[...] = tails.astype(BF16)
+
+    pl.semaphore_wait(barrier, 22)
     tail_copy = neighbour(tail_s, tail_r, 0, following)
     tail_copy.start()
-    send_all(0, block_of(taps_h), taps_r, 7, 16)
+    send_all(0, block_of(taps_h), taps_r)
     for n in range(3, 6):
         loads[n].wait()
 
@@ -199,20 +197,22 @@
 
             first = short_filter(x1, 0)
             grad = go[rows, :]
-            pair_s[h, block, 0] = (grad.astype(F32) * first).astype(BF16)
+            grad_gate = (grad.astype(F32) * first).astype(BF16)
+            pair_s[h, block, 0] = grad_gate
             second = short_filter(x2, 1)
             value = short_filter(xv, 2)
             act2[rows, :] = second
             actv[rows, :] = value
-            pair_s[h, block, 1] = (second * value).astype(BF16)
+            gated = (second * value).astype(BF16)
+            pair_s[h, block, 1] = gated
             spot = pl.ds(multiple(block * 16, 16), 16)
-            head_tile[h, 0, spot, :] = pair_s[h, block, 1, :, 0:128]
-            head_tile[h, 1, spot, :] = pair_s[h, block, 0, :, 0:128]
+            head_tile[h, 0, spot, :] = gated[:, 0:128]
+            head_tile[h, 1, spot, :] = grad_gate[:, 0:128]
             head_tile[h, 2, spot, :] = grad[:, 0:128]
             head_tile[h, 3, spot, :] = value[:, 0:128].astype(BF16)
             head_tile[h, 4, spot, :] = second[:, 0:128].astype(BF16)
 
-        loop(0, 16, body)
+        unrolled(0, 16, body)
 
     for h in range(2):
         gate(h)
@@ -404,7 +404,7 @@
             filter_out()
         mixes_out(h)
 
-    def adjoint(h):
+    def adjoint(h, sums):
         wait_bytes(mm_r.at[h], recv_sem.at[4 + h])
 
         def body(block):
@@ -432,9 +432,11 @@
                 )
                 out[rows, :] = full.astype(BF16)
                 total += stream[rows, :].astype(F32) * full
-            sal_s[...] += total[0:8] + total[8:16]
-
-        loop(0, 16, body)
+            return total[0:8] + total[8:16]
+
+        for block in range(16):
+            sums = sums + body(block)
+        return sums
 
     loads[16].wait()
     swap_in = neighbour(sk_h, sk.at[1 - core], 2, sibling)
@@ -449,7 +451,6 @@
 
     unrolled(0, 4, sketch_rows)
     send_all(6, slot_of(part_s), rs_r)
-    sal_s[...] = jnp.zeros((8, 512), F32)
     head_copy.wait_recv()
     for h in range(2):
         heads = head_r[h].astype(F32) * (me < 15).astype(F32)
@@ -457,8 +458,7 @@
         head_gate[h] = jnp.transpose(wrow[:, 0:256])
         wrow[0:16, 0:256] = pltpu.roll(heads, 10, 0)
         head_mult[h] = jnp.transpose(wrow[:, 0:256])
-    adjoint(0)
-    adjoint(1)
+    sal_s[...] = adjoint(1, adjoint(0, jnp.zeros((8, 512), F32)))
     outs = [
         pltpu.make_async_copy(a, b, out_sem.at[n])
         for n, (a, b) in enumerate(((o1, o1_h), (o2, o2_h), (ov, ov_h), (osk, osk_h), (osal, osal_h)))

time: 65.5 us -> 61.8 us (0.944)
  Pallas kernels: 64.5 us -> 60.8 us
    pallas_call x1, Pallas kernels: 61.1 us -> 57.3 us  [on_device(): pl.pallas_call(kernel, out_shape=[*[jax.ShapeDtypeStruct(square, BF16) fo...]
where the time goes in v5:
time: 61.8 us; the launch traced here: 61.6 us
  Pallas kernels  60.8 us (98%)
  between operations  0.8 us (1%)
    pallas_call x1, Pallas kernels, on_device(): pl.pallas_call(kernel, out_shape=[*[jax.ShapeDtypeStruct(square, BF16) fo...  57.3 us
    pallas_call x1, Pallas kernels, on_device(): pl.pallas_call(finish, out_shape=[*[jax.ShapeDtypeStruct(square, BF16) fo...  3.47 us

profile of v5, /device:TPU:1, one launch (start us, length us, event | category | flops | bytes accessed | tf_op | source)
XLA Modules:
  0.0 61.6 jit_solution(12719522666763128777)
XLA Ops:
  0.6 57.3 %shard_map.209 = (bf16[512,512]{1,0:T(8,128)(2,1)}, bf16[512,512]{1,0:T(8,128)(2,1)}, bf16[512,512]{1,0:T(8,128)(2,1)}, f32[8,128]{1,0:T(8,128)}, f32[64,512]{1,0:T(8,128)}) custom-call(bf16[512,512]{1,0:T(8,128)(2,1)} %x1_h.1, bf16[512,512]{1,0:T(8,128)(2,1)} %x2_h.1, bf16[512,512]{1,0:T(8,128)(2,1)} %xv_h.1, bf16[512,512]{1,0:T(8,128)(2,1)} %go_h.1, ...), custom_call_target="tpu_custom_call" | custom-call | tf_op jit(solution)/shard_map/pallas_call | solution.py:558
  58.0 3.5 %shard_map.210 = (bf16[512,512]{1,0:T(8,128)(2,1)}, bf16[512,512]{1,0:T(8,128)(2,1)}, bf16[512,512]{1,0:T(8,128)(2,1)}, f32[64]{0:T(128)}, f32[64,512]{1,0:T(8,128)}) custom-call(bf16[512,512]{1,0:T(8,128)(2,1)} %get-tuple-element.10.a1, bf16[512,512]{1,0:T(8,128)(2,1)} %get-tuple-element.11.a2, bf16[512,512]{1,0:T(8,128)(2,1)} %get-tuple-element.12.av, ...), custom_call_target="tpu_custom_call" | custom-call | tf_op jit(solution)/shard_map/pallas_call | solution.py:573

commit v6 on v5

--- a/solution.py
+++ b/solution.py
@@ -438,19 +438,6 @@
             sums = sums + body(block)
         return sums
 
-    loads[16].wait()
-    swap_in = neighbour(sk_h, sk.at[1 - core], 2, sibling)
-    swap_in.wait_recv()
-    wait_bytes(gf_s, recv_sem.at[3])
-
-    def sketch_rows(block):
-        rows = pl.ds(block * 256, 256)
-        total = dot_nt(sk[0, rows, :], gf_r[:, 0].reshape(256, 512))
-        total += dot_nt(sk[1, rows, :], gf_r[:, 1].reshape(256, 512))
-        part_s[pl.ds(block * 4, 4)] = total.astype(BF16).reshape(4, 64, 256)
-
-    unrolled(0, 4, sketch_rows)
-    send_all(6, slot_of(part_s), rs_r)
     head_copy.wait_recv()
     for h in range(2):
         heads = head_r[h].astype(F32) * (me < 15).astype(F32)
@@ -458,7 +445,22 @@
         head_gate[h] = jnp.transpose(wrow[:, 0:256])
         wrow[0:16, 0:256] = pltpu.roll(heads, 10, 0)
         head_mult[h] = jnp.transpose(wrow[:, 0:256])
-    sal_s[...] = adjoint(1, adjoint(0, jnp.zeros((8, 512), F32)))
+    sums = adjoint(0, jnp.zeros((8, 512), F32))
+
+    loads[16].wait()
+    swap_in = neighbour(sk_h, sk.at[1 - core], 2, sibling)
+    swap_in.wait_recv()
+    wait_bytes(gf_s, recv_sem.at[3])
+
+    def sketch_rows(block):
+        rows = pl.ds(block * 256, 256)
+        total = dot_nt(sk[0, rows, :], gf_r[:, 0].reshape(256, 512))
+        total += dot_nt(sk[1, rows, :], gf_r[:, 1].reshape(256, 512))
+        part_s[pl.ds(block * 4, 4)] = total.astype(BF16).reshape(4, 64, 256)
+
+    unrolled(0, 4, sketch_rows)
+    send_all(6, slot_of(part_s), rs_r)
+    sal_s[...] = adjoint(1, sums)
     outs = [
         pltpu.make_async_copy(a, b, out_sem.at[n])
         for n, (a, b) in enumerate(((o1, o1_h), (o2, o2_h), (ov, ov_h), (osk, osk_h), (osal, osal_h)))

time: 61.8 us -> 61.8 us (level)
  no operation moved by 1% of the time
where the time goes in v6:
time: 61.8 us; the launch traced here: 61.6 us
  Pallas kernels  60.8 us (98%)
  between operations  0.8 us (1%)
    pallas_call x1, Pallas kernels, on_device(): pl.pallas_call(kernel, out_shape=[*[jax.ShapeDtypeStruct(square, BF16) fo...  57.3 us
    pallas_call x1, Pallas kernels, on_device(): pl.pallas_call(finish, out_shape=[*[jax.ShapeDtypeStruct(square, BF16) fo...  3.47 us

profile of v6, /device:TPU:1, one launch (start us, length us, event | category | flops | bytes accessed | tf_op | source)
XLA Modules:
  0.0 61.6 jit_solution(14172046297579924607)
XLA Ops:
  0.6 57.3 %shard_map.209 = (bf16[512,512]{1,0:T(8,128)(2,1)}, bf16[512,512]{1,0:T(8,128)(2,1)}, bf16[512,512]{1,0:T(8,128)(2,1)}, f32[8,128]{1,0:T(8,128)}, f32[64,512]{1,0:T(8,128)}) custom-call(bf16[512,512]{1,0:T(8,128)(2,1)} %x1_h.1, bf16[512,512]{1,0:T(8,128)(2,1)} %x2_h.1, bf16[512,512]{1,0:T(8,128)(2,1)} %xv_h.1, bf16[512,512]{1,0:T(8,128)(2,1)} %go_h.1, ...), custom_call_target="tpu_custom_call" | custom-call | tf_op jit(solution)/shard_map/pallas_call | solution.py:560
  58.0 3.5 %shard_map.210 = (bf16[512,512]{1,0:T(8,128)(2,1)}, bf16[512,512]{1,0:T(8,128)(2,1)}, bf16[512,512]{1,0:T(8,128)(2,1)}, f32[64]{0:T(128)}, f32[64,512]{1,0:T(8,128)}) custom-call(bf16[512,512]{1,0:T(8,128)(2,1)} %get-tuple-element.10.a1, bf16[512,512]{1,0:T(8,128)(2,1)} %get-tuple-element.11.a2, bf16[512,512]{1,0:T(8,128)(2,1)} %get-tuple-element.12.av, ...), custom_call_target="tpu_custom_call" | custom-call | tf_op jit(solution)/shard_map/pallas_call | solution.py:575
